TPU v7x, 512 devices: a whole 4x4x16 slice. The times are simulated.
512 devices in a mesh: seq: 32 (over x, y, core), head: 16 (over z).
Axes of the slice: x: 4, y: 4, z: 16, core: 2. Of those that a mesh axis runs over, the one named last changes fastest.
Arguments:
- queries: bfloat16 [4096, 8192], P('seq', 'head'), may hold values from -6 to 6
- keys: bfloat16 [4096, 1024], P('seq'), may hold values from -6 to 6
- values: bfloat16 [4096, 1024], P('seq'), may hold values from -6 to 6
- doc_lengths: int32 [12], replicated, may hold values from 1 to 2048, 4096 in all
- fq_weight: bfloat16 [64, 128, 128], P('head'), may hold values from -1 to 1
- fk_weight: bfloat16 [64, 128, 128], P('head'), may hold values from -1 to 1
Outputs:
- residual: float32 [4096, 8192], P('seq', 'head')
- token_loss: float32 [4096], P('seq')
Inputs may be any that keep to these rules, and one draw needn't show every extreme that they name: `doc_lengths`: the 12 documents are packed in order and their lengths sum to 4096; the longest has exactly 2048 tokens.
All inputs are finite; a program needn't handle non-finite values.
Results may differ from a plain program's by a relative error of at most 0.0035.
Values may be sent and summed in bfloat16 or wider, within the bound.
No kernel may reach another device: no remote copies, remote signals or barrier semaphores. Data moves between devices by JAX's collectives and lax.ppermute only.
A program may use at most 64 MiB of HBM per device.

v0:
```python
import jax
import jax.numpy as jnp
from jax import lax
from jax.sharding import Mesh
from jax.sharding import PartitionSpec as P

QH = 64
KVH = 8
SEQ = ("seq_0", "seq_1", "seq_2")


NEG = -1e30


def laid_out(parts, dim):
    dims = list(parts.shape[1:])
    dims[dim] *= parts.shape[0]
    return jnp.moveaxis(parts, 0, dim).reshape(dims)


def from_everyone(array, axis):
    copies = jnp.broadcast_to(array, (lax.axis_size(axis), *array.shape))
    return lax.all_to_all(copies, axis, split_axis=0, concat_axis=0, tiled=True)


def gather_directly(array, axis, dim):
    return laid_out(from_everyone(array, axis), dim)


def side_by_side(arrays, axis, dim, along):
    ends, at = ([], 0)
    for a in arrays[:-1]:
        at += a.shape[along]
        ends.append(at)
    both = jnp.concatenate(arrays, axis=along)
    return tuple(jnp.split(gather_directly(both, axis, dim), ends, axis=along))


def nothing_yet(array, identity):
    return jax.tree.map(
        lambda part, zero: jnp.zeros_like(part) + jnp.asarray(zero, part.dtype), array, identity
    )


def entering(array, axes, combine, identity):
    before = start = nothing_yet(array, identity)
    total = array
    for axis in reversed(axes):
        length, index = (lax.axis_size(axis), lax.axis_index(axis))
        pieces = jax.tree.map(
            lambda part, kind: lax.all_gather(part.astype(kind), axis),
            total,
            (jnp.bfloat16, jnp.bfloat16, jnp.bfloat16),
        )
        inside, total = (start, start)
        for k in range(length):
            passed = k < index
            total = combine(
                total, jax.tree.map(lambda part, own: part[k].astype(own.dtype), pieces, array)
            )
            inside = jax.tree.map(lambda new, old: jnp.where(passed, new, old), total, inside)
        before = combine(inside, before)
    return before


def taken_together(array, axis):
    everything = from_everyone(array, axis)
    return jnp.sum(everything, axis=0)


def doc_index(positions, starts):
    return jnp.sum((starts[None, :] <= positions[:, None]).astype(jnp.int32), axis=1) - 1


def feature_map(projected):
    return jnp.concatenate(
        [jax.nn.softmax(projected, axis=-1), jax.nn.softmax(-projected, axis=-1)], axis=-1
    ).astype(jnp.bfloat16)


def chain(earlier, later):
    return (
        earlier[0] * later[0],
        later[1] + later[0] * earlier[1],
        later[2] + later[0] * earlier[2],
    )


def body(queries, keys, values, doc_lengths, fq_weight, fk_weight):
    tok_rows = queries.shape[0]
    heads = fq_weight.shape[0]
    head_dim = fq_weight.shape[1]
    group = QH // KVH
    kv_local = max(1, heads // group)
    repeat = heads // kv_local
    kv_first = lax.axis_index("head") * heads // group
    k_own = lax.dynamic_slice_in_dim(keys, kv_first * head_dim, kv_local * head_dim, 1)
    v_own = lax.dynamic_slice_in_dim(values, kv_first * head_dim, kv_local * head_dim, 1)
    starts = jnp.cumsum(doc_lengths) - doc_lengths
    anchor = lax.axis_index(SEQ) * tok_rows
    q_pos = anchor + jnp.arange(tok_rows, dtype=jnp.int32)
    q_doc = doc_index(q_pos, starts)
    query_groups = queries.reshape(tok_rows, kv_local, repeat, head_dim)
    first_start = jnp.max(jnp.where(starts <= anchor, starts, 0))
    last_pos = anchor + tok_rows - 1
    scale = head_dim ** (-0.5)
    init = (
        jnp.full((kv_local, repeat, tok_rows), NEG, jnp.float32),
        jnp.zeros((kv_local, repeat, tok_rows), jnp.float32),
        jnp.zeros((kv_local, repeat, tok_rows, head_dim), jnp.float32),
    )
    pieces = side_by_side((k_own, v_own), SEQ, 0, 1)
    start = jnp.int32(0)
    rows = pieces[0].shape[0]
    needed = (start <= last_pos) & (start + rows - 1 >= first_start)

    def compute(state):
        peak, total, accum = state
        key_segment = pieces[0].reshape(rows, kv_local, head_dim)
        v_piece = pieces[1].reshape(rows, kv_local, head_dim)
        k_pos = jnp.arange(rows, dtype=jnp.int32)
        k_doc = doc_index(k_pos, starts)
        mask = (
            (q_doc[:, None] == k_doc[None, :])
            & (k_pos[None, :] <= q_pos[:, None])
            & (k_pos[None, :] >= 0)
        )
        scores = jnp.where(
            mask,
            jnp.einsum(
                "caju,iau->ajci", query_groups, key_segment, preferred_element_type=jnp.float32
            )
            * scale,
            NEG,
        )
        new_peak = jnp.maximum(peak, jnp.max(scores, axis=-1))
        weights = jnp.exp(scores - new_peak[..., None])
        total = jnp.sum(weights, axis=-1)
        accum = jnp.einsum(
            "xebw,wxy->xeby",
            weights.astype(jnp.bfloat16),
            v_piece,
            preferred_element_type=jnp.float32,
        )
        return (new_peak, total, accum)

    peak, total, accum = lax.cond(needed, compute, lambda state: state, init)
    teacher = accum / total[..., None]
    k_grouped = k_own.reshape(tok_rows, kv_local, head_dim)
    value_groups = v_own.reshape(tok_rows, kv_local, head_dim)
    query_feature_map = feature_map(
        jnp.einsum(
            "tgrd,grdf->tgrf",
            query_groups,
            fq_weight.reshape(kv_local, repeat, head_dim, -1),
            preferred_element_type=jnp.float32,
        )
    )
    key_feature_map = feature_map(
        jnp.einsum(
            "tgd,grdf->tgrf",
            k_grouped,
            fk_weight.reshape(kv_local, repeat, head_dim, -1),
            preferred_element_type=jnp.float32,
        )
    )
    local_mask = (q_doc[:, None] == q_doc[None, :]) & (q_pos[None, :] <= q_pos[:, None])
    score_matrix = jnp.where(
        local_mask,
        jnp.einsum(
            "dbpj,zbpj->bpdz",
            query_feature_map,
            key_feature_map,
            preferred_element_type=jnp.float32,
        ),
        0.0,
    )
    numer = jnp.einsum(
        "xebw,wxy->xeby",
        score_matrix,
        value_groups.astype(jnp.float32),
        precision=lax.Precision.HIGHEST,
    )
    denom = jnp.sum(score_matrix, axis=-1)
    last_mask = (q_doc == q_doc[-1]).astype(jnp.bfloat16)
    phi_last = key_feature_map * last_mask[:, None, None, None]
    state = jnp.einsum("sgrf,sgd->grfd", phi_last, value_groups, preferred_element_type=jnp.float32)
    norm_state = jnp.sum(phi_last.astype(jnp.float32), axis=0)
    inside = jnp.sum(((starts >= anchor) & (starts < anchor + tok_rows)).astype(jnp.int32))
    keep = (inside == 0).astype(jnp.float32)
    identity = (jnp.ones((), jnp.float32), jnp.zeros_like(state), jnp.zeros_like(norm_state))
    running_prefix = entering((keep, state, norm_state), SEQ, chain, identity)
    prev_doc = doc_index(jnp.reshape(anchor - 1, (1,)), starts)[0]
    carried = (q_doc == prev_doc).astype(jnp.float32)
    widened_feature_map = query_feature_map.astype(jnp.float32)
    numer = numer + carried[None, None, :, None] * jnp.einsum(
        "tgrf,grfd->grtd", widened_feature_map, running_prefix[1], precision=lax.Precision.HIGHEST
    )
    denom = denom + carried[None, None, :] * jnp.einsum(
        "skqa,kqa->kqs", widened_feature_map, running_prefix[2], precision=lax.Precision.HIGHEST
    )
    student = numer / denom[..., None]
    difference = teacher - student
    residual = jnp.transpose(difference, (2, 0, 1, 3)).reshape(tok_rows, heads * head_dim)
    local_loss = jnp.sum(jnp.mean(difference * difference, axis=-1), axis=(0, 1))
    token_loss = taken_together(local_loss, "head")
    return (residual, token_loss)


def solution(mesh):
    split = Mesh(
        mesh.devices.reshape(4, 4, 2, mesh.shape["head"]), ("seq_0", "seq_1", "seq_2", "head")
    )
    placed = (
        P(SEQ, "head"),
        P(SEQ, None),
        P(SEQ, None),
        P(),
        P("head", None, None),
        P("head", None, None),
    )
    return jax.shard_map(
        body, mesh=split, in_specs=placed, out_specs=(P(SEQ, "head"), P(SEQ)), check_vma=False
    )
```

profile of v0, /device:TPU:24, one launch (start us, length us, event | category | flops | bytes accessed | tf_op | source)
XLA Modules:
  0.0 183.2 jit_solution(1631600980179276708)
XLA Ops:
  7.3 0.8 reduce-window.9
  8.1 1.4 fusion.99
  10.2 1.3 dynamic-slice
  11.5 0.7 dynamic-update-slice
  12.8 2.5 %all-reduce = bf16[2]{0:T(256)(128)(2,1)S(1)} all-reduce(bf16[2]{0:T(256)(128)(2,1)S(1)} %dynamic-update-slice), channel_id=1, replica_groups=mesh['seq_0'=4,'seq_1'=4,'seq_2'=2,'head'=16] {'seq_2'}, use_global_device_ids=true, to_apply=%add | all-reduce | flops 2 | bytes 8
  17.3 1.0 copy.52
  18.4 0.8 constant_dynamic-slice_fusion
  20.5 2.2 %all-gather = bf16[8,256,128]{2,1,0:T(8,128)(2,1)S(1)} all-gather(bf16[4,256,128]{2,1,0:T(8,128)(2,1)S(1)} %convolution_convert_fusion), channel_id=2, replica_groups=mesh['seq_0'=4,'seq_1'=4,'seq_2'=2,'head'=16] {'seq_2'}, dimensions={0}, use_global_device_ids=true | all-gather | bytes 786432 | tf_op jit(solution)/shard_map/all_gather | solution.py:51
  23.3 0.8 fusion.43
  25.5 1.3 dynamic-slice.1
  27.4 12.1 %all-reduce.1 = bf16[4]{0:T(256)(128)(2,1)S(1)} all-reduce(bf16[4]{0:T(256)(128)(2,1)S(1)} %dynamic-update-slice.1), channel_id=1, replica_groups=mesh['seq_0'=4,'seq_1'=4,'seq_2'=2,'head'=16] {'seq_1'}, use_global_device_ids=true, to_apply=%add.1 | all-reduce | flops 4 | bytes 16
  39.5 1.3 dynamic-slice.2
  44.0 0.8 dynamic-update-slice.2
  44.8 1.6 broadcast_in_dim.80
  46.4 4.9 %all-to-all-start = ((bf16[32,128,256]{2,1,0:T(8,128)(2,1)}), bf16[32,128,256]{2,1,0:T(8,128)(2,1)S(1)}, u32[]{:S(2)}, u32[]{:S(2)}) async-start(bf16[32,128,256]{2,1,0:T(8,128)(2,1)} %broadcast_in_dim.80), calls=%async_computation | async-start | bytes 4194304 | tf_op jit(solution)/shard_map/all_to_all | solution.py:23
  51.4 28.9 %all-reduce.2 = bf16[4]{0:T(256)(128)(2,1)S(1)} all-reduce(bf16[4]{0:T(256)(128)(2,1)S(1)} %dynamic-update-slice.2), channel_id=1, replica_groups=mesh['seq_0'=4,'seq_1'=4,'seq_2'=2,'head'=16] {'seq_0'}, use_global_device_ids=true, to_apply=%add.2 | all-reduce | flops 4 | bytes 16
  88.0 1.8 all-gather.2
  89.8 10.1 %all_gather.58 = bf16[4,1,4,256]{3,2,1,0:T(4,128)(2,1)S(1)} all-gather(bf16[1,1,4,256]{3,2,1,0:T(4,128)(2,1)S(1)} %fusion.96), channel_id=1, replica_groups=mesh['seq_0'=4,'seq_1'=4,'seq_2'=2,'head'=16] {'seq_1'}, dimensions={0}, use_global_device_ids=true | all-gather | bytes 10240 | tf_op jit(solution)/shard_map/all_gather | solution.py:51
  100.0 10.4 %all_gather.59 = bf16[4,1,4,256]{3,2,1,0:T(4,128)(2,1)S(1)} all-gather(bf16[1,1,4,256]{3,2,1,0:T(4,128)(2,1)S(1)} %get-tuple-element.63), channel_id=1, replica_groups=mesh['seq_0'=4,'seq_1'=4,'seq_2'=2,'head'=16] {'seq_0'}, dimensions={0}, use_global_device_ids=true | all-gather | bytes 10240 | tf_op jit(solution)/shard_map/all_gather | solution.py:51
  110.3 2.1 %fusion.35 = bf16[1,1,4,256,128]{4,3,2,1,0:T(8,128)(2,1)} fusion(f32[]{:T(128)S(6)} %convert.45, f32[]{:T(128)S(6)} %convert.44, f32[]{:T(128)S(6)} %mul.331, f32[]{:T(128)S(6)} %convert.43, bf16[4,1,4,256,128]{4,3,2,1,0:T(8,128)(2,1)} %all-gather.6.cloned.1.call-done), kind=kLoop, calls=%fused_computation.51 | loop fusion | flops 1572864 | bytes 1310736 | tf_op jit(solution)/shard_map/convert_element_type | solution.py:51
  113.3 1.0 fusion.112
  114.3 5.8 %conditional.1 = (f32[1,4,128]{2,1,0:T(4,128)S(1)}, f32[1,4,128,128]{2,3,1,0:T(8,128)S(1)}) conditional(s32[]{:T(128)} %convert_element_type.347, () %tuple.19, (s32[128]{0:T(128)S(1)}, s32[12]{0:T(128)S(1)}, s32[]{:T(128)}, s32[128]{0:T(128)S(1)}, bf16[32,128,256]{2,1,0:T(8,128)(2,1)S(1)}, /*index=5*/bf16[128,512]{1,0:T(8,128)(2,1)S(1)}) %tuple.57), branch_computations={%region_3.4_spmd, %region_4.8_spmd} | conditional | flops 1090141824 | bytes 28784708 | solution.py:147
  114.5 1.9 %fusion.6 = pred[128,4096]{0,1:T(8,128)(4,1)S(1)} fusion(s32[128]{0:T(128)S(1)} %broadcast_add_fusion.1, s32[128]{0:T(128)S(1)} %get-tuple-element.31, s32[4096]{0:T(1024)S(1)} %broadcast_add_fusion), kind=kLoop, calls=%fused_computation.8 | loop fusion | flops 1572864 | bytes 541696 | tf_op jit(solution)/shard_map/cond/branch_1_fun/and | solution.py:124
  116.4 1.3 fusion.108
  117.7 1.3 fusion.7
  119.0 1.1 fusion.1
  120.1 26.3 %all-gather.8.cloned.1.call-done = bf16[4,1,4,256,128]{4,3,2,1,0:T(8,128)(2,1)} async-done(((bf16[1,1,4,256,128]{4,3,2,1,0:T(8,128)(2,1)}), bf16[4,1,4,256,128]{4,3,2,1,0:T(8,128)(2,1)}) %all-gather.8.cloned.1.call-update) | async-done | bytes 1048592 | tf_op jit(solution)/shard_map/all_gather | solution.py:51
  146.4 2.8 %convolution_multiply_fusion = f32[4,128,128]{1,2,0:T(8,128)S(1)} fusion(bf16[4,1,4,256,128]{4,3,2,1,0:T(8,128)(2,1)} %all-gather.8.cloned.1.call-done, f32[]{:T(128)S(6)} %convert.41, f32[]{:T(128)S(6)} %mul.323, f32[]{:T(128)S(6)} %mul.339, f32[]{:T(128)S(6)} %select_n.254, f32[]{:T(128)S(6)} %convert.46, f32[]{:T(128)S(6)} %convert.45, f32[]{:T(128)S(6)} %convert.47, ...), kind=kOutput, calls=%fused_computation.20 | convolution fusion | flops 207290368 | bytes 3146298 | tf_op jit(solution)/shard_map/tgrf,grfd->grtd/dot_general | solution.py:196
  149.2 1.3 multiply_reduce_fusion
  151.2 12.3 %all-to-all-start.1 = ((f32[16,1,128]{2,1,0:T(1,128)}), f32[16,1,128]{2,1,0:T(1,128)S(1)}, u32[]{:S(2)}, u32[]{:S(2)}) async-start(f32[16,1,128]{2,1,0:T(1,128)} %broadcast_in_dim.89), calls=%async_computation.1 | async-start | bytes 16384 | tf_op jit(solution)/shard_map/all_to_all | solution.py:23
  163.5 0.8 copy.60
  164.3 11.5 %all-to-all-done.1 = f32[16,1,128]{2,1,0:T(1,128)S(1)} async-done(((f32[16,1,128]{2,1,0:T(1,128)}), f32[16,1,128]{2,1,0:T(1,128)S(1)}, u32[]{:S(2)}, u32[]{:S(2)}) %all-to-all-start.1) | async-done | bytes 8224 | tf_op jit(solution)/shard_map/all_to_all | solution.py:23
  (46 shorter events, 7.1 us)
Async XLA Ops:
  7.2 105.3 %copy-start = (bf16[4,128,128]{2,1,0:T(8,128)(2,1)S(1)}, bf16[4,128,128]{2,1,0:T(8,128)(2,1)}, u32[]{:S(2)}) copy-start(bf16[4,128,128]{2,1,0:T(8,128)(2,1)} %param.12) | copy-start | bytes 393220
  7.2 105.3 %copy-start.1 = (bf16[128,512]{1,0:T(8,128)(2,1)S(1)}, bf16[128,512]{1,0:T(8,128)(2,1)}, u32[]{:S(2)}) copy-start(bf16[128,512]{1,0:T(8,128)(2,1)} %param.8) | copy-start | bytes 393220
  7.2 103.2 %all-gather.6.cloned.1.call-start = ((), (), s32[]{:S(2)}) async-start(), calls=%async_computation.2 | async-start | bytes 1310720 | tf_op jit(solution)/shard_map/all_gather | solution.py:51
  46.4 67.9 %all-to-all-start = ((bf16[32,128,256]{2,1,0:T(8,128)(2,1)}), bf16[32,128,256]{2,1,0:T(8,128)(2,1)S(1)}, u32[]{:S(2)}, u32[]{:S(2)}) async-start(bf16[32,128,256]{2,1,0:T(8,128)(2,1)} %broadcast_in_dim.80), calls=%async_computation | async-start | bytes 4194304 | tf_op jit(solution)/shard_map/all_to_all | solution.py:23
  51.3 95.1 %all-gather.8.cloned.1.call-start = ((), (), s32[]{:S(2)}) async-start(), calls=%async_computation.3 | async-start | bytes 1310720 | tf_op jit(solution)/shard_map/all_gather | solution.py:51
  151.2 24.7 %all-to-all-start.1 = ((f32[16,1,128]{2,1,0:T(1,128)}), f32[16,1,128]{2,1,0:T(1,128)S(1)}, u32[]{:S(2)}, u32[]{:S(2)}) async-start(f32[16,1,128]{2,1,0:T(1,128)} %broadcast_in_dim.89), calls=%async_computation.1 | async-start | bytes 16384 | tf_op jit(solution)/shard_map/all_to_all | solution.py:23
Sparse Core Ops, SparseCore 0:
  24.3 56.3 all-gather.5
  112.6 33.8 all-gather.7
where the time goes:
time: 184 us; the launch traced here: 183 us
  blocking collectives  67.9 us (37%)
  waiting for transfers between devices  37.9 us (21%)
  between operations  27.6 us (15%)
  starting transfers between devices  17.3 us (9%)
  local copies, waits for them, and re-layouts  13.5 us (7%)
  other arithmetic  10.4 us (6%)
  matrix products  8.54 us (5%)
    unnamed x3, blocking collectives  43.5 us
    all_gather x2, waiting for transfers between devices, entering(): lax.all_gather(part.astype(kind), axis)  26.3 us
    all_gather x4, blocking collectives, entering(): lax.all_gather(part.astype(kind), axis)  24.5 us
    all_to_all x2, starting transfers between devices, from_everyone(): return lax.all_to_all(copies, axis, split_axis=0, concat_axis=0, tiled=True)  17.2 us
    all_to_all x2, waiting for transfers between devices, from_everyone(): return lax.all_to_all(copies, axis, split_axis=0, concat_axis=0, tiled=True)  11.5 us
    unnamed x15, local copies, waits for them, and re-layouts  7.91 us
  transfers between devices with their start and end apart: 4, of which 2 were waited for; matrix products, arithmetic and copies ran while one was open for 10% of the time, Pallas kernels for 0%

commit v1 on v0

v1 whole, which is shorter than its diff:
```python
import math

import jax
import jax.numpy as jnp
from jax import lax
from jax.experimental import pallas as pl
from jax.experimental.pallas import tpu as pltpu
from jax.sharding import Mesh
from jax.sharding import PartitionSpec as P

QH = 64
KVH = 8
MAXDOC = 2048
CHIP = ("seq_0", "seq_1")
CORE = "seq_2"
SEQ = (*CHIP, CORE)
NEG = -1e30
LOG2E = math.log2(math.e)
NT = (((1,), (1,)), ((), ()))


def dot(a, b, dims=(((1,), (0,)), ((), ()))):
    return lax.dot_general(a, b, dims, preferred_element_type=jnp.float32)


def split_dot(a, b):
    high = a.astype(jnp.bfloat16)
    low = (a - high.astype(jnp.float32)).astype(jnp.bfloat16)
    return dot(high, b) + dot(low, b)


def doc_start(doc_ref, pos):
    start = jnp.zeros_like(pos)
    at = jnp.int32(0)
    for d in range(doc_ref.shape[0]):
        start = jnp.where(pos >= at, at, start)
        at = at + doc_ref[d]
    return start


def softmaxes(proj, axis):
    p = proj * LOG2E
    up = jnp.exp2(p - jnp.max(p, axis=axis, keepdims=True))
    down = jnp.exp2(jnp.min(p, axis=axis, keepdims=True) - p)
    up = up * (1.0 / jnp.sum(up, axis=axis, keepdims=True))
    down = down * (1.0 / jnp.sum(down, axis=axis, keepdims=True))
    return jnp.concatenate([up.astype(jnp.bfloat16), down.astype(jnp.bfloat16)], axis=axis)


def with_ones(v):
    return jnp.concatenate([v, jnp.ones_like(v)], axis=1)


def own_kernel(at_ref, doc_ref, q_ref, k_ref, v_ref, fq_ref, fk_ref, lhs_ref, sd_ref, phi_ref, nd_ref):
    heads, hd, _ = fq_ref.shape
    rows = q_ref.shape[0]
    anchor = (2 * at_ref[0] + at_ref[1]) * rows
    q_pos = anchor + lax.broadcasted_iota(jnp.int32, (rows, 1), 0)
    k_pos = anchor + lax.broadcasted_iota(jnp.int32, (1, rows), 1)
    mask = (k_pos >= doc_start(doc_ref, q_pos)) & (k_pos <= q_pos)
    k = k_ref[...]
    v = with_ones(v_ref[...])
    for h in range(heads):
        q = q_ref[:, h * hd:(h + 1) * hd]
        lhs_ref[h * rows:(h + 1) * rows, :] = q
        fk_t = jnp.transpose(fk_ref[h].astype(jnp.float32)).astype(jnp.bfloat16)
        lhs_ref[heads * rows + h * hd:heads * rows + (h + 1) * hd, :] = fk_t
        sd_ref[h] = jnp.where(mask, dot(q, k, NT) * (hd ** -0.5 * LOG2E), NEG)
        phi_q = softmaxes(dot(q, fq_ref[h]), 1)
        phi_ref[h] = phi_q
        phi_k = softmaxes(dot(fk_t, k, NT), 0)
        affinity = jnp.where(mask, dot(phi_q, phi_k), 0.0)
        nd_ref[h] = split_dot(affinity, v)


def earlier_kernel(
    at_ref, doc_ref, a_ref, b_ref, lhs_ref, sd_ref, phi_ref, nd_ref, res_ref, loss_ref,
    s_scr, state_scr, max_scr, acc_scr,
):
    heads, rows, hd = sd_ref.shape
    chip, core = at_ref[0], at_ref[1]
    anchor = (2 * chip + core) * rows
    first = doc_start(doc_ref, anchor)
    c0 = first // (2 * rows)
    c1 = jnp.where(first < anchor, (anchor - 1) // (2 * rows) + 1, c0)
    qr = heads * rows
    scale = hd ** -0.5 * LOG2E
    state_scr[...] = jnp.zeros_like(state_scr)
    acc_scr[...] = jnp.zeros_like(acc_scr)
    max_scr[...] = jnp.full_like(max_scr, NEG)

    def positions(c, shape, dim):
        lane = lax.broadcasted_iota(jnp.int32, shape, dim)
        own = (2 * c + core) * rows + lane
        other = (2 * c + 1 - core) * rows + lane - rows
        pos = jnp.where(lane < rows, own, other)
        return (pos >= first) & (pos < anchor)

    def both(c, at):
        return jnp.concatenate([a_ref[c, :, at:at + hd], b_ref[c, :, at:at + hd]], axis=0)

    def scan_keys(c, _):
        z = dot(lhs_ref[...], both(c, 0), NT)
        s = jnp.where(positions(c, (1, 2 * rows), 1), z[:qr] * scale, NEG)
        s_scr[c - c0] = s
        max_scr[...] = jnp.maximum(max_scr[...], jnp.maximum(s[:, :rows], s[:, rows:]))
        seen = jnp.where(positions(c, (2 * rows, 1), 0), 1.0, 0.0).astype(jnp.bfloat16)
        v = with_ones(both(c, hd)) * seen
        for h in range(heads):
            phi_k = softmaxes(z[qr + h * hd:qr + (h + 1) * hd], 0)
            state_scr[h] += dot(phi_k, v)
        return _

    lax.fori_loop(c0, c1, scan_keys, 0)

    q_pos = anchor + lax.broadcasted_iota(jnp.int32, (rows, 1), 0)
    carried = jnp.broadcast_to(jnp.where(doc_start(doc_ref, q_pos) == first, 1.0, 0.0), (rows, hd)) > 0.5
    v_own = with_ones(a_ref[chip, :, hd:2 * hd])
    for h in range(heads):
        at = slice(h * rows, (h + 1) * rows)
        sd = sd_ref[h]
        off = jnp.broadcast_to(jnp.max(max_scr[at], axis=1, keepdims=True), (rows, hd))
        peak = jnp.maximum(
            jnp.broadcast_to(jnp.max(sd, axis=1, keepdims=True), (rows, hd)), jnp.where(carried, off, NEG)
        )
        acc_scr[at] = dot(jnp.exp2(sd - peak).astype(jnp.bfloat16), v_own)
        max_scr[at] = jnp.where(carried, peak, -NEG)

    def weigh(c, _):
        peak = max_scr[...]
        s = s_scr[c - c0]
        w = jnp.concatenate(
            [jnp.exp2(s[:, :rows] - peak).astype(jnp.bfloat16), jnp.exp2(s[:, rows:] - peak).astype(jnp.bfloat16)],
            axis=1,
        )
        acc_scr[...] += dot(w, with_ones(both(c, hd)))
        return _

    lax.fori_loop(c0, c1, weigh, 0)

    squares = jnp.zeros((rows, hd), jnp.float32)
    for h in range(heads):
        acc = acc_scr[h * rows:(h + 1) * rows]
        state = state_scr[h]
        high = state.astype(jnp.bfloat16)
        low = (state - high.astype(jnp.float32)).astype(jnp.bfloat16)
        phi = phi_ref[h]
        nd = dot(phi, high) + dot(phi, low)
        own = nd_ref[h]
        numer = own[:, :hd] + jnp.where(carried, nd[:, :hd], 0.0)
        denom = own[:, hd:] + jnp.where(carried, nd[:, hd:], 0.0)
        residual = acc[:, :hd] / acc[:, hd:] - numer / denom
        res_ref[:, h * hd:(h + 1) * hd] = residual
        squares = squares + residual * residual
    loss = jnp.sum(jnp.transpose(squares), axis=0, keepdims=True) * (1.0 / hd)
    loss_ref[...] = jnp.broadcast_to(loss, loss_ref.shape)


def body(queries, keys, values, doc_lengths, fq_weight, fk_weight):
    rows = queries.shape[0]
    heads, hd, _ = fq_weight.shape
    kv_head = lax.axis_index("head") * heads // (QH // KVH)
    chip, core = lax.axis_index(CHIP), lax.axis_index(CORE)
    chips, planes = lax.axis_size(CHIP), lax.axis_size("head")
    at = jnp.stack([chip, core]).astype(jnp.int32)
    k_own = lax.dynamic_slice_in_dim(keys, kv_head * hd, hd, 1)
    v_own = lax.dynamic_slice_in_dim(values, kv_head * hd, hd, 1)
    kv = jnp.concatenate([k_own, v_own], axis=1)
    a = lax.all_to_all(jnp.broadcast_to(kv, (chips, *kv.shape)), CHIP, 0, 0, tiled=True)
    b = lax.ppermute(a, CORE, [(0, 1), (1, 0)])
    smem = pl.BlockSpec(memory_space=pltpu.SMEM)
    vmem = pl.BlockSpec(memory_space=pltpu.VMEM)
    params = pltpu.CompilerParams(vmem_limit_bytes=32 * 1024 * 1024)
    f32, bf16 = jnp.float32, jnp.bfloat16
    lhs, sd, phi, nd = pl.pallas_call(
        own_kernel,
        out_shape=(
            jax.ShapeDtypeStruct((heads * (rows + hd), hd), bf16),
            jax.ShapeDtypeStruct((heads, rows, rows), f32),
            jax.ShapeDtypeStruct((heads, rows, 2 * hd), bf16),
            jax.ShapeDtypeStruct((heads, rows, 2 * hd), f32),
        ),
        in_specs=[smem, smem] + [vmem] * 5,
        out_specs=(vmem,) * 4,
        compiler_params=params,
        cost_estimate=pl.CostEstimate(flops=10**9, bytes_accessed=2 * 10**6, transcendentals=10**6),
        name="own_block",
    )(at, doc_lengths, queries, k_own, v_own, fq_weight, fk_weight)
    steps = MAXDOC // (2 * rows) + 1
    residual, loss = pl.pallas_call(
        earlier_kernel,
        out_shape=(
            jax.ShapeDtypeStruct((rows, heads * hd), f32),
            jax.ShapeDtypeStruct((planes, rows), f32),
        ),
        in_specs=[smem, smem] + [vmem] * 6,
        out_specs=(vmem, vmem),
        scratch_shapes=[
            pltpu.VMEM((steps, heads * rows, 2 * rows), f32),
            pltpu.VMEM((heads, 2 * hd, 2 * hd), f32),
            pltpu.VMEM((heads * rows, rows), f32),
            pltpu.VMEM((heads * rows, 2 * hd), f32),
        ],
        compiler_params=params,
        cost_estimate=pl.CostEstimate(flops=4 * 10**9, bytes_accessed=4 * 10**6, transcendentals=4 * 10**6),
        name="earlier_blocks",
    )(at, doc_lengths, a, b, lhs, sd, phi, nd)
    parts = lax.all_to_all(loss, "head", 0, 0, tiled=True)
    return residual, jnp.sum(parts, axis=0)


def solution(mesh):
    split = Mesh(mesh.devices.reshape(4, 4, 2, mesh.shape["head"]), (*SEQ, "head"))
    placed = (
        P(SEQ, "head"),
        P(SEQ, None),
        P(SEQ, None),
        P(),
        P("head", None, None),
        P("head", None, None),
    )
    return jax.shard_map(
        body, mesh=split, in_specs=placed, out_specs=(P(SEQ, "head"), P(SEQ)), check_vma=False
    )
```

time: 184 us -> 67.1 us (0.36)
  the two profiles are of different devices: /device:TPU:24 before, /device:TPU:7 now
where the time goes in v1:
time: 67.1 us; the launch traced here: 66.8 us
  blocking collectives  46.3 us (69%)
  Pallas kernels  13 us (19%)
  starting transfers between devices  4.72 us (7%)
  local copies, waits for them, and re-layouts  1.47 us (2%)
  between operations  0.73 us (1%)
    all_to_all x1, blocking collectives, body(): parts = lax.all_to_all(loss, 'head', 0, 0, tiled=True)  26 us
    all_to_all x1, blocking collectives, body(): lax.all_to_all(jnp.broadcast_to(kv, (chips, *kv.shape)), CHIP, 0, 0, tile...  20.3 us
    pallas_call x1, Pallas kernels, body(): pl.pallas_call(earlier_kernel, out_shape=(jax.ShapeDtypeStruct((rows, hea...  10.6 us
    ppermute x1, starting transfers between devices, body(): b = lax.ppermute(a, CORE, [(0, 1), (1, 0)])  4.72 us
    pallas_call x1, Pallas kernels, body(): pl.pallas_call(own_kernel, out_shape=(jax.ShapeDtypeStruct((heads * (rows...  2.33 us
  transfers between devices with their start and end apart: 1, of which 0 were waited for; matrix products, arithmetic and copies ran while one was open for 0% of the time, Pallas kernels for 3%

profile of v1, /device:TPU:7, one launch (start us, length us, event | category | flops | bytes accessed | tf_op | source)
XLA Modules:
  0.0 66.8 jit_solution(12121849659010256548)
XLA Ops:
  0.7 0.8 %constant_dynamic-slice_fusion = (bf16[128,128]{1,0:T(8,128)(2,1)S(1)}, bf16[128,128]{1,0:T(8,128)(2,1)S(1)}) fusion(bf16[128,1024]{1,0:T(8,128)(2,1)} %param.8, s32[]{:T(128)S(6)} %select_n.10, bf16[128,1024]{1,0:T(8,128)(2,1)} %param.7), kind=kLoop, calls=%fused_computation.2 | loop fusion | bytes 131076 | tf_op jit(solution)/shard_map/dynamic_slice | solution.py:167
  1.4 0.1 broadcast_in_dim.3
  1.6 0.0 copy-start
  1.6 0.0 copy-start.1
  1.6 0.0 copy-start.2
  1.6 20.3 %all_to_all.14.a_ref = bf16[16,128,256]{2,1,0:T(8,128)(2,1)S(1)} all-to-all(bf16[16,128,256]{2,1,0:T(8,128)(2,1)S(1)} %broadcast_in_dim.3), channel_id=1, replica_groups=mesh['seq_0'=4,'seq_1'=4,'seq_2'=2,'head'=16] {'seq_0','seq_1'}, dimensions={0} | all-to-all | bytes 2097152 | tf_op jit(solution)/shard_map/all_to_all | solution.py:169
  21.9 4.7 %collective-permute-start = (bf16[16,128,256]{2,1,0:T(8,128)(2,1)S(1)}, bf16[16,128,256]{2,1,0:T(8,128)(2,1)S(1)}, u32[]{:S(2)}, u32[]{:S(2)}) collective-permute-start(bf16[16,128,256]{2,1,0:T(8,128)(2,1)S(1)} %all_to_all.14.a_ref), channel_id=1, source_target_pairs={{0,16},{16,0},{1,17},{17,1},{2,18},{18,2},{3,19},{19,3},{4,20},{20... | collective-permute-start | bytes 3145736 | tf_op jit(solution)/shard_map/ppermute | solution.py:170
  26.6 0.0 copy-start.3
  26.6 0.1 pad_add_fusion.at_ref
  26.7 0.0 copy-done
  26.7 0.0 copy-done.1
  26.7 0.0 copy-done.2
  26.7 0.6 copy-done.3
  27.3 2.3 %own_block.1 = (bf16[1024,128]{1,0:T(8,128)(2,1)S(1)}, f32[4,128,128]{2,1,0:T(8,128)S(1)}, bf16[4,128,256]{2,1,0:T(8,128)(2,1)S(1)}, f32[4,128,256]{2,1,0:T(8,128)S(1)}) custom-call(s32[2]{0:T(128)S(1)} %pad_add_fusion.at_ref, s32[12]{0:T(128)S(1)} %copy-done.3, bf16[128,512]{1,0:T(8,128)(2,1)S(1)} %copy-done, bf16[128,128]{1,0:T(8,128)(2,1)S(1)} %get-tuple-element.15.k_ref, ...), custom_call_target="tpu_custom_call" | custom-call | flops 1000000000 | bytes 2000000 | tf_op jit(solution)/shard_map/own_block/pallas_call | solution.py:175
  29.6 0.0 collective-permute-done.b_ref
  29.6 10.6 %earlier_blocks.1 = (f32[128,512]{1,0:T(8,128)}, f32[16,128]{1,0:T(8,128)S(1)}) custom-call(s32[2]{0:T(128)S(1)} %pad_add_fusion.at_ref, s32[12]{0:T(128)S(1)} %copy-done.3, bf16[16,128,256]{2,1,0:T(8,128)(2,1)S(1)} %all_to_all.14.a_ref, bf16[16,128,256]{2,1,0:T(8,128)(2,1)S(1)} %collective-permute-done.b_ref, ...), custom_call_target="tpu_custom_call" | custom-call | flops 4000000000 | bytes 4000000 | tf_op jit(solution)/shard_map/earlier_blocks/pallas_call | solution.py:190
  40.2 26.0 %all_to_all.15 = f32[16,1,128]{2,1,0:T(1,128)S(1)} all-to-all(f32[16,1,128]{2,1,0:T(1,128)S(1)} %bitcast.5), channel_id=1, replica_groups=mesh['seq_0'=4,'seq_1'=4,'seq_2'=2,'head'=16] {'head'}, dimensions={0} | all-to-all | bytes 16384 | tf_op jit(solution)/shard_map/all_to_all | solution.py:208
  66.3 0.5 reduce_sum.9
  (1 shorter events, 0.0 us)
Async XLA Ops:
  1.6 25.1 %copy-start = (bf16[128,512]{1,0:T(8,128)(2,1)S(1)}, bf16[128,512]{1,0:T(8,128)(2,1)}, u32[]{:S(2)}) copy-start(bf16[128,512]{1,0:T(8,128)(2,1)} %q_ref.1) | copy-start | bytes 393220
  1.6 25.1 %copy-start.1 = (bf16[4,128,128]{2,1,0:T(8,128)(2,1)S(1)}, bf16[4,128,128]{2,1,0:T(8,128)(2,1)}, u32[]{:S(2)}) copy-start(bf16[4,128,128]{2,1,0:T(8,128)(2,1)} %fq_ref.1) | copy-start | bytes 393220
  1.6 25.1 %copy-start.2 = (bf16[4,128,128]{2,1,0:T(8,128)(2,1)S(1)}, bf16[4,128,128]{2,1,0:T(8,128)(2,1)}, u32[]{:S(2)}) copy-start(bf16[4,128,128]{2,1,0:T(8,128)(2,1)} %fk_ref.1) | copy-start | bytes 393220
  21.9 7.7 %collective-permute-start = (bf16[16,128,256]{2,1,0:T(8,128)(2,1)S(1)}, bf16[16,128,256]{2,1,0:T(8,128)(2,1)S(1)}, u32[]{:S(2)}, u32[]{:S(2)}) collective-permute-start(bf16[16,128,256]{2,1,0:T(8,128)(2,1)S(1)} %all_to_all.14.a_ref), channel_id=1, source_target_pairs={{0,16},{16,0},{1,17},{17,1},{2,18},{18,2},{3,19},{19,3},{4,20},{20... | collective-permute-start | bytes 3145736 | tf_op jit(solution)/shard_map/ppermute | solution.py:170
  26.6 0.7 copy-start.3

commit v2 on v1

v2 whole, which is shorter than its diff:
```python
import math

import jax
import jax.numpy as jnp
from jax import lax
from jax.experimental import pallas as pl
from jax.experimental.pallas import tpu as pltpu
from jax.sharding import Mesh
from jax.sharding import PartitionSpec as P

QH = 64
KVH = 8
MAXDOC = 2048
CHIP = ("seq_0", "seq_1")
CORE = "seq_2"
SEQ = (*CHIP, CORE)
NEG = -1e30
LOG2E = math.log2(math.e)
NT = (((1,), (1,)), ((), ()))


def dot(a, b, dims=(((1,), (0,)), ((), ()))):
    return lax.dot_general(a, b, dims, preferred_element_type=jnp.float32)


def split_dot(a, b):
    high = a.astype(jnp.bfloat16)
    low = (a - high.astype(jnp.float32)).astype(jnp.bfloat16)
    return dot(high, b) + dot(low, b)


def doc_start(doc_ref, pos):
    start = jnp.zeros_like(pos)
    at = jnp.int32(0)
    for d in range(doc_ref.shape[0]):
        start = jnp.where(pos >= at, at, start)
        at = at + doc_ref[d]
    return start


def softmaxes(proj, axis):
    p = proj * LOG2E
    up = jnp.exp2(p - jnp.max(p, axis=axis, keepdims=True))
    down = jnp.exp2(jnp.min(p, axis=axis, keepdims=True) - p)
    up = up * (1.0 / jnp.sum(up, axis=axis, keepdims=True))
    down = down * (1.0 / jnp.sum(down, axis=axis, keepdims=True))
    return jnp.concatenate([up.astype(jnp.bfloat16), down.astype(jnp.bfloat16)], axis=axis)


def with_ones(v):
    return jnp.concatenate([v, jnp.ones_like(v)], axis=1)


def send_kernel(k_ref, v_ref, send_ref):
    hd = k_ref.shape[1]
    k_t = jnp.transpose(k_ref[...].astype(jnp.float32)).astype(jnp.bfloat16)
    for c in range(send_ref.shape[0]):
        send_ref[c, :, :hd] = k_t
        send_ref[c, :, hd:] = v_ref[...]


def own_kernel(at_ref, doc_ref, q_ref, k_ref, v_ref, fq_ref, fk_ref, lhs_ref, sd_ref, phi_ref, nd_ref, v_own_ref):
    heads, hd, _ = fq_ref.shape
    rows = q_ref.shape[0]
    anchor = (2 * at_ref[0] + at_ref[1]) * rows
    q_pos = anchor + lax.broadcasted_iota(jnp.int32, (rows, 1), 0)
    k_pos = anchor + lax.broadcasted_iota(jnp.int32, (1, rows), 1)
    mask = (k_pos >= doc_start(doc_ref, q_pos)) & (k_pos <= q_pos)
    k = k_ref[...]
    v = with_ones(v_ref[...])
    v_own_ref[...] = v
    for h in range(heads):
        q = q_ref[:, h * hd:(h + 1) * hd]
        lhs_ref[h * rows:(h + 1) * rows, :] = q
        fk_t = jnp.transpose(fk_ref[h].astype(jnp.float32)).astype(jnp.bfloat16)
        lhs_ref[heads * rows + h * hd:heads * rows + (h + 1) * hd, :] = fk_t
        sd_ref[h] = jnp.where(mask, dot(q, k, NT) * (hd ** -0.5 * LOG2E), NEG)
        phi_q = softmaxes(dot(q, fq_ref[h]), 1)
        phi_ref[h] = phi_q
        phi_k = softmaxes(dot(fk_t, k, NT), 0)
        affinity = jnp.where(mask, dot(phi_q, phi_k), 0.0)
        nd_ref[h] = split_dot(affinity, v)


def scan_keys(kv_ref, lhs_ref, s_ref, max_ref, state_ref, c0, parity, first, anchor, before):
    heads, rows, hd = state_ref.shape[0], max_ref.shape[1], kv_ref.shape[1]
    qr = heads * rows
    scale = hd ** -0.5 * LOG2E

    def visible(c, shape, dim):
        lane = lax.broadcasted_iota(jnp.int32, shape, dim)
        pos = (2 * c + parity) * rows + lane + jnp.where(lane < rows, 0, rows)
        return (pos >= first) & (pos < anchor)

    for i in range(s_ref.shape[0]):
        c = c0 + 2 * i
        low, high = jnp.maximum(c, 0), jnp.maximum(c + 1, 0)
        k_t = jnp.concatenate([kv_ref[low, :, :hd], kv_ref[high, :, :hd]], axis=1)
        v = jnp.concatenate([kv_ref[low, :, hd:], kv_ref[high, :, hd:]], axis=0)
        z = dot(lhs_ref[...], k_t)
        s = jnp.where(visible(c, (1, 2 * rows), 1), z[:qr] * scale, NEG)
        s_ref[i] = s
        m = jnp.maximum(s[:, :rows], s[:, rows:])
        if i > 0:
            m = jnp.maximum(max_ref[...], m)
        elif before is not None:
            m = jnp.maximum(before[0][...], m)
        max_ref[...] = m
        v = with_ones(v) * jnp.where(visible(c, (2 * rows, 1), 0), 1.0, 0.0).astype(jnp.bfloat16)
        for h in range(heads):
            d = dot(softmaxes(z[qr + h * hd:qr + (h + 1) * hd], 0), v)
            if i > 0:
                d = state_ref[h] + d
            elif before is not None:
                d = before[1][h] + d
            state_ref[h] = d


def same_core_kernel(at_ref, doc_ref, a_ref, lhs_ref, s_ref, max_ref, state_ref):
    rows = max_ref.shape[1]
    chip, core = at_ref[0], at_ref[1]
    anchor = (2 * chip + core) * rows
    first = doc_start(doc_ref, anchor)
    scan_keys(a_ref, lhs_ref, s_ref, max_ref, state_ref, chip - 2 * s_ref.shape[0], core, first, anchor, None)


def other_core_kernel(
    at_ref, doc_ref, a_ref, b_ref, lhs_ref, sa_ref, max_a_ref, state_a_ref, sd_ref, phi_ref, nd_ref, v_own_ref,
    res_ref, loss_ref, sb_ref, max_ref, state_ref, acc_ref,
):
    heads, rows, hd = sd_ref.shape
    chip, core = at_ref[0], at_ref[1]
    anchor = (2 * chip + core) * rows
    first = doc_start(doc_ref, anchor)
    steps = sb_ref.shape[0]
    a0, b0 = chip - 2 * steps, chip - 2 * steps + core
    scan_keys(b_ref, lhs_ref, sb_ref, max_ref, state_ref, b0, 1 - core, first, anchor, (max_a_ref, state_a_ref))

    q_pos = anchor + lax.broadcasted_iota(jnp.int32, (rows, 1), 0)
    carried = jnp.broadcast_to(jnp.where(doc_start(doc_ref, q_pos) == first, 1.0, 0.0), (rows, hd)) > 0.5
    for h in range(heads):
        at = slice(h * rows, (h + 1) * rows)
        sd = sd_ref[h]
        off = jnp.broadcast_to(jnp.max(max_ref[at], axis=1, keepdims=True), (rows, hd))
        peak = jnp.maximum(
            jnp.broadcast_to(jnp.max(sd, axis=1, keepdims=True), (rows, hd)), jnp.where(carried, off, NEG)
        )
        acc_ref[at] = dot(jnp.exp2(sd - peak).astype(jnp.bfloat16), v_own_ref[...])
        max_ref[at] = jnp.where(carried, peak, -NEG)

    weights, seen = [], []
    for kv_ref, s_ref, c0 in ((a_ref, sa_ref, a0), (b_ref, sb_ref, b0)):
        for i in range(steps):
            c = c0 + 2 * i
            low, high = jnp.maximum(c, 0), jnp.maximum(c + 1, 0)
            peak = max_ref[...]
            s = s_ref[i]
            weights.append(jnp.exp2(s[:, :rows] - peak).astype(jnp.bfloat16))
            weights.append(jnp.exp2(s[:, rows:] - peak).astype(jnp.bfloat16))
            seen.append(with_ones(kv_ref[low, :, hd:]))
            seen.append(with_ones(kv_ref[high, :, hd:]))
    acc_ref[...] += dot(jnp.concatenate(weights, axis=1), jnp.concatenate(seen, axis=0))

    squares = jnp.zeros((rows, hd), jnp.float32)
    for h in range(heads):
        acc = acc_ref[h * rows:(h + 1) * rows]
        state = state_ref[h]
        high = state.astype(jnp.bfloat16)
        low = (state - high.astype(jnp.float32)).astype(jnp.bfloat16)
        phi = phi_ref[h]
        nd = dot(phi, high) + dot(phi, low)
        own = nd_ref[h]
        numer = own[:, :hd] + jnp.where(carried, nd[:, :hd], 0.0)
        denom = own[:, hd:] + jnp.where(carried, nd[:, hd:], 0.0)
        residual = acc[:, :hd] / acc[:, hd:] - numer / denom
        res_ref[:, h * hd:(h + 1) * hd] = residual
        squares = squares + residual * residual
    loss = jnp.sum(jnp.transpose(squares), axis=0, keepdims=True) * (1.0 / hd)
    loss_ref[...] = jnp.broadcast_to(loss, loss_ref.shape)


F32, BF16 = jnp.float32, jnp.bfloat16
SMEM = pl.BlockSpec(memory_space=pltpu.SMEM)
VMEM = pl.BlockSpec(memory_space=pltpu.VMEM)


def shapes(*items):
    return tuple(jax.ShapeDtypeStruct(s, t) for s, t in items)


def params(mib):
    return pltpu.CompilerParams(vmem_limit_bytes=mib * 1024 * 1024)


def to_send(k_own, v_own, chips):
    rows, hd = k_own.shape
    return pl.pallas_call(
        send_kernel,
        out_shape=jax.ShapeDtypeStruct((chips, hd, rows + hd), BF16),
        in_specs=[VMEM, VMEM],
        out_specs=VMEM,
        compiler_params=params(8),
        name="to_send",
    )(k_own, v_own)


def own_block(at, doc_lengths, queries, k_own, v_own, fq_weight, fk_weight):
    rows = queries.shape[0]
    heads, hd, _ = fq_weight.shape
    return pl.pallas_call(
        own_kernel,
        out_shape=shapes(
            ((heads * (rows + hd), hd), BF16),
            ((heads, rows, rows), F32),
            ((heads, rows, 2 * hd), BF16),
            ((heads, rows, 2 * hd), F32),
            ((rows, 2 * hd), BF16),
        ),
        in_specs=[SMEM, SMEM] + [VMEM] * 5,
        out_specs=(VMEM,) * 5,
        compiler_params=params(16),
        cost_estimate=pl.CostEstimate(flops=10**9, bytes_accessed=2 * 10**6, transcendentals=10**6),
        name="own_block",
    )(at, doc_lengths, queries, k_own, v_own, fq_weight, fk_weight)


def same_core(at, doc_lengths, a, lhs, heads):
    rows = hd = lhs.shape[1]
    steps = MAXDOC // (4 * rows)
    return pl.pallas_call(
        same_core_kernel,
        out_shape=shapes(
            ((steps, heads * rows, 2 * rows), F32), ((heads * rows, rows), F32), ((heads, 2 * hd, 2 * hd), F32)
        ),
        in_specs=[SMEM, SMEM, VMEM, VMEM],
        out_specs=(VMEM,) * 3,
        compiler_params=params(16),
        cost_estimate=pl.CostEstimate(flops=2 * 10**9, bytes_accessed=4 * 10**6, transcendentals=2 * 10**6),
        name="same_core",
    )(at, doc_lengths, a, lhs)


def other_core(at, doc_lengths, a, b, lhs, sa, max_a, state_a, sd, phi, nd, v_own, planes):
    heads, rows, hd = sd.shape
    return pl.pallas_call(
        other_core_kernel,
        out_shape=shapes(((rows, heads * hd), F32), ((planes, rows), F32)),
        in_specs=[SMEM, SMEM] + [VMEM] * 10,
        out_specs=(VMEM, VMEM),
        scratch_shapes=[
            pltpu.VMEM(sa.shape, F32),
            pltpu.VMEM(max_a.shape, F32),
            pltpu.VMEM(state_a.shape, F32),
            pltpu.VMEM((heads * rows, 2 * hd), F32),
        ],
        compiler_params=params(24),
        cost_estimate=pl.CostEstimate(flops=4 * 10**9, bytes_accessed=4 * 10**6, transcendentals=4 * 10**6),
        name="other_core",
    )(at, doc_lengths, a, b, lhs, sa, max_a, state_a, sd, phi, nd, v_own)


def body(queries, keys, values, doc_lengths, fq_weight, fk_weight):
    heads, hd, _ = fq_weight.shape
    kv_head = lax.axis_index("head") * heads // (QH // KVH)
    at = jnp.stack([lax.axis_index(CHIP), lax.axis_index(CORE)]).astype(jnp.int32)
    k_own = lax.dynamic_slice_in_dim(keys, kv_head * hd, hd, 1)
    v_own = lax.dynamic_slice_in_dim(values, kv_head * hd, hd, 1)
    send = to_send(k_own, v_own, lax.axis_size(CHIP))
    a = lax.all_to_all(send, CHIP, 0, 0, tiled=True)
    lhs, sd, phi, nd, v_own = own_block(at, doc_lengths, queries, k_own, v_own, fq_weight, fk_weight)
    a, lhs = lax.optimization_barrier((a, lhs))
    b = lax.ppermute(a, CORE, [(0, 1), (1, 0)])
    sa, max_a, state_a = same_core(at, doc_lengths, a, lhs, heads)
    residual, loss = other_core(
        at, doc_lengths, a, b, lhs, sa, max_a, state_a, sd, phi, nd, v_own, lax.axis_size("head")
    )
    parts = lax.all_to_all(loss, "head", 0, 0, tiled=True)
    return residual, jnp.sum(parts, axis=0)


def solution(mesh):
    split = Mesh(mesh.devices.reshape(4, 4, 2, mesh.shape["head"]), (*SEQ, "head"))
    placed = (
        P(SEQ, "head"),
        P(SEQ, None),
        P(SEQ, None),
        P(),
        P("head", None, None),
        P("head", None, None),
    )
    return jax.shard_map(
        body, mesh=split, in_specs=placed, out_specs=(P(SEQ, "head"), P(SEQ)), check_vma=False
    )
```

time: 67.1 us -> 64.7 us (0.964)
  the two profiles are of different devices: /device:TPU:7 before, /device:TPU:1 now
where the time goes in v2:
time: 64.7 us; the launch traced here: 64.4 us
  blocking collectives  26.6 us (41%)
  starting transfers between devices  13.3 us (21%)
  waiting for transfers between devices  11.8 us (18%)
  Pallas kernels  10.5 us (16%)
  local copies, waits for them, and re-layouts  0.88 us (1%)
  between operations  0.74 us (1%)
    all_to_all x1, blocking collectives, body(): parts = lax.all_to_all(loss, 'head', 0, 0, tiled=True)  26.6 us
    all_to_all x1, waiting for transfers between devices, body(): a = lax.all_to_all(send, CHIP, 0, 0, tiled=True)  11.8 us
    all_to_all x1, starting transfers between devices, body(): a = lax.all_to_all(send, CHIP, 0, 0, tiled=True)  7.58 us
    ppermute x1, starting transfers between devices, body(): b = lax.ppermute(a, CORE, [(0, 1), (1, 0)])  5.73 us
    pallas_call x1, Pallas kernels, other_core(): pl.pallas_call(other_core_kernel, out_shape=shapes(((rows, heads * hd), F...  4.46 us
    pallas_call x1, Pallas kernels, same_core(): pl.pallas_call(same_core_kernel, out_shape=shapes(((steps, heads * rows,...  2.56 us
    pallas_call x1, Pallas kernels, own_block(): pl.pallas_call(own_kernel, out_shape=shapes(((heads * (rows + hd), hd), B...  2.33 us
  transfers between devices with their start and end apart: 2, of which 1 were waited for; matrix products, arithmetic and copies ran while one was open for 0% of the time, Pallas kernels for 8%

profile of v2, /device:TPU:1, one launch (start us, length us, event | category | flops | bytes accessed | tf_op | source)
XLA Modules:
  0.0 64.4 jit_solution(5836770889985482130)
XLA Ops:
  0.6 0.0 copy-start.3
  0.6 0.0 copy-start.2
  0.7 0.0 copy-start.1
  0.7 0.0 copy-start
  0.7 0.9 %constant_dynamic-slice_fusion = (bf16[128,128]{1,0:T(8,128)(2,1)S(1)}, bf16[128,128]{1,0:T(8,128)(2,1)S(1)}) fusion(bf16[128,1024]{1,0:T(8,128)(2,1)} %param.8, s32[]{:T(128)S(6)} %select_n.10, bf16[128,1024]{1,0:T(8,128)(2,1)} %param.7), kind=kLoop, calls=%fused_computation.1 | loop fusion | bytes 131076 | tf_op jit(solution)/shard_map/dynamic_slice | solution.py:267
  1.6 1.1 %to_send.1 = bf16[16,128,256]{2,1,0:T(8,128)(2,1)} custom-call(bf16[128,128]{1,0:T(8,128)(2,1)S(1)} %get-tuple-element.27.k_ref, bf16[128,128]{1,0:T(8,128)(2,1)S(1)} %get-tuple-element.26.v_ref), custom_call_target="tpu_custom_call" | custom-call | tf_op jit(solution)/shard_map/to_send/pallas_call | solution.py:197
  2.7 7.6 %all-to-all-start = ((bf16[16,128,256]{2,1,0:T(8,128)(2,1)}), bf16[16,128,256]{2,1,0:T(8,128)(2,1)S(1)}, u32[]{:S(2)}, u32[]{:S(2)}) async-start(bf16[16,128,256]{2,1,0:T(8,128)(2,1)} %to_send.1), calls=%async_computation | async-start | bytes 2097152 | tf_op jit(solution)/shard_map/all_to_all | solution.py:269
  10.3 0.1 pad_add_fusion.at_ref
  10.4 0.0 copy-done.3
  10.4 0.0 copy-done.2
  10.4 0.0 copy-done.1
  10.4 0.0 copy-done
  10.4 2.3 %own_block.1 = (bf16[1024,128]{1,0:T(8,128)(2,1)S(1)}, f32[4,128,128]{2,1,0:T(8,128)S(1)}, bf16[4,128,256]{2,1,0:T(8,128)(2,1)S(1)}, f32[4,128,256]{2,1,0:T(8,128)S(1)}, bf16[128,256]{1,0:T(8,128)(2,1)S(1)}) custom-call(s32[2]{0:T(128)S(1)} %pad_add_fusion.at_ref, s32[12]{0:T(128)S(1)} %copy-done.3, bf16[128,512]{1,0:T(8,128)(2,1)S(1)} %copy-done, ...), custom_call_target="tpu_custom_call" | custom-call | flops 1000000000 | bytes 2000000 | tf_op jit(solution)/shard_map/own_block/pallas_call | solution.py:210
  12.7 11.8 %all-to-all-done.a_ref = bf16[16,128,256]{2,1,0:T(8,128)(2,1)S(1)} async-done(((bf16[16,128,256]{2,1,0:T(8,128)(2,1)}), bf16[16,128,256]{2,1,0:T(8,128)(2,1)S(1)}, u32[]{:S(2)}, u32[]{:S(2)}) %all-to-all-start) | async-done | bytes 1048608 | tf_op jit(solution)/shard_map/all_to_all | solution.py:269
  24.5 5.7 %collective-permute-start = (bf16[16,128,256]{2,1,0:T(8,128)(2,1)S(1)}, bf16[16,128,256]{2,1,0:T(8,128)(2,1)S(1)}, u32[]{:S(2)}, u32[]{:S(2)}) collective-permute-start(bf16[16,128,256]{2,1,0:T(8,128)(2,1)S(1)} %all-to-all-done.a_ref), channel_id=1, source_target_pairs={{0,16},{16,0},{1,17},{17,1},{2,18},{18,2},{3,19},{19,3},{4,20},{20... | collective-permute-start | bytes 3145736 | tf_op jit(solution)/shard_map/ppermute | solution.py:272
  30.3 2.6 %same_core.1 = (f32[4,512,256]{2,1,0:T(8,128)S(1)}, f32[512,128]{1,0:T(8,128)S(1)}, f32[4,256,256]{2,1,0:T(8,128)S(1)}) custom-call(s32[2]{0:T(128)S(1)} %pad_add_fusion.at_ref, s32[12]{0:T(128)S(1)} %copy-done.3, bf16[16,128,256]{2,1,0:T(8,128)(2,1)S(1)} %all-to-all-done.a_ref, bf16[1024,128]{1,0:T(8,128)(2,1)S(1)} %get-tuple-element.16.lhs_ref), custom_call_target="tpu_custom_call" | custom-call | flops 2000000000 | bytes 4000000 | tf_op jit(solution)/shard_map/same_core/pallas_call | solution.py:230
  32.8 0.0 collective-permute-done.b_ref
  32.8 4.5 %other_core.1 = (f32[128,512]{1,0:T(8,128)}, f32[16,128]{1,0:T(8,128)S(1)}) custom-call(s32[2]{0:T(128)S(1)} %pad_add_fusion.at_ref, s32[12]{0:T(128)S(1)} %copy-done.3, bf16[16,128,256]{2,1,0:T(8,128)(2,1)S(1)} %all-to-all-done.a_ref, bf16[16,128,256]{2,1,0:T(8,128)(2,1)S(1)} %collective-permute-done.b_ref, ...), custom_call_target="tpu_custom_call" | custom-call | flops 4000000000 | bytes 4000000 | tf_op jit(solution)/shard_map/other_core/pallas_call | solution.py:245
  37.3 26.6 %all_to_all.14 = f32[16,1,128]{2,1,0:T(1,128)S(1)} all-to-all(f32[16,1,128]{2,1,0:T(1,128)S(1)} %bitcast.5), channel_id=1, replica_groups=mesh['seq_0'=4,'seq_1'=4,'seq_2'=2,'head'=16] {'head'}, dimensions={0} | all-to-all | bytes 16384 | tf_op jit(solution)/shard_map/all_to_all | solution.py:277
  63.9 0.5 reduce_sum.9
Async XLA Ops:
  0.6 9.8 %copy-start.3 = (s32[12]{0:T(128)S(1)}, s32[12]{0:T(128)}, u32[]{:S(2)}) copy-start(s32[12]{0:T(128)} %doc_ref.5) | copy-start | bytes 148
  0.6 9.7 %copy-start.2 = (bf16[4,128,128]{2,1,0:T(8,128)(2,1)S(1)}, bf16[4,128,128]{2,1,0:T(8,128)(2,1)}, u32[]{:S(2)}) copy-start(bf16[4,128,128]{2,1,0:T(8,128)(2,1)} %fk_ref.1) | copy-start | bytes 393220
  0.7 9.7 %copy-start.1 = (bf16[4,128,128]{2,1,0:T(8,128)(2,1)S(1)}, bf16[4,128,128]{2,1,0:T(8,128)(2,1)}, u32[]{:S(2)}) copy-start(bf16[4,128,128]{2,1,0:T(8,128)(2,1)} %fq_ref.1) | copy-start | bytes 393220
  0.7 9.7 %copy-start = (bf16[128,512]{1,0:T(8,128)(2,1)S(1)}, bf16[128,512]{1,0:T(8,128)(2,1)}, u32[]{:S(2)}) copy-start(bf16[128,512]{1,0:T(8,128)(2,1)} %q_ref.1) | copy-start | bytes 393220
  2.7 21.8 %all-to-all-start = ((bf16[16,128,256]{2,1,0:T(8,128)(2,1)}), bf16[16,128,256]{2,1,0:T(8,128)(2,1)S(1)}, u32[]{:S(2)}, u32[]{:S(2)}) async-start(bf16[16,128,256]{2,1,0:T(8,128)(2,1)} %to_send.1), calls=%async_computation | async-start | bytes 2097152 | tf_op jit(solution)/shard_map/all_to_all | solution.py:269
  24.5 8.3 %collective-permute-start = (bf16[16,128,256]{2,1,0:T(8,128)(2,1)S(1)}, bf16[16,128,256]{2,1,0:T(8,128)(2,1)S(1)}, u32[]{:S(2)}, u32[]{:S(2)}) collective-permute-start(bf16[16,128,256]{2,1,0:T(8,128)(2,1)S(1)} %all-to-all-done.a_ref), channel_id=1, source_target_pairs={{0,16},{16,0},{1,17},{17,1},{2,18},{18,2},{3,19},{19,3},{4,20},{20... | collective-permute-start | bytes 3145736 | tf_op jit(solution)/shard_map/ppermute | solution.py:272

commit v3 on v2

--- a/solution.py
+++ b/solution.py
@@ -8,25 +8,27 @@
 from jax.sharding import Mesh
 from jax.sharding import PartitionSpec as P
 
-QH = 64
-KVH = 8
 MAXDOC = 2048
 CHIP = ("seq_0", "seq_1")
 CORE = "seq_2"
 SEQ = (*CHIP, CORE)
 NEG = -1e30
+FIRST_CHIP, FIRST_PLANE = 10, 8
 LOG2E = math.log2(math.e)
-NT = (((1,), (1,)), ((), ()))
-
-
-def dot(a, b, dims=(((1,), (0,)), ((), ()))):
-    return lax.dot_general(a, b, dims, preferred_element_type=jnp.float32)
+
+
+def dot(a, b):
+    return jnp.dot(a, b, preferred_element_type=jnp.float32)
 
 
 def split_dot(a, b):
     high = a.astype(jnp.bfloat16)
     low = (a - high.astype(jnp.float32)).astype(jnp.bfloat16)
     return dot(high, b) + dot(low, b)
+
+
+def slot(c, chips):
+    return lax.rem(jnp.maximum(c, 0) + (chips - FIRST_CHIP), chips)
 
 
 def doc_start(doc_ref, pos):
@@ -51,33 +53,46 @@
     return jnp.concatenate([v, jnp.ones_like(v)], axis=1)
 
 
-def send_kernel(k_ref, v_ref, send_ref):
-    hd = k_ref.shape[1]
-    k_t = jnp.transpose(k_ref[...].astype(jnp.float32)).astype(jnp.bfloat16)
-    for c in range(send_ref.shape[0]):
-        send_ref[c, :, :hd] = k_t
-        send_ref[c, :, hd:] = v_ref[...]
-
-
-def own_kernel(at_ref, doc_ref, q_ref, k_ref, v_ref, fq_ref, fk_ref, lhs_ref, sd_ref, phi_ref, nd_ref, v_own_ref):
+def send_kernel(keys_ref, values_ref, send_ref, own_ref, k_ref, in_sem, out_sem):
+    chips, hd, _ = send_ref.shape
+    rows = k_ref.shape[0]
+    column = lax.axis_index("head") * keys_ref.shape[1] // (hd * lax.axis_size("head"))
+    at = pl.ds(pl.multiple_of(column * hd, hd), hd)
+    get_k = pltpu.make_async_copy(keys_ref.at[:, at], k_ref, in_sem.at[0])
+    get_v = pltpu.make_async_copy(values_ref.at[:, at], own_ref.at[:, pl.ds(rows, hd)], in_sem.at[1])
+    get_k.start()
+    get_v.start()
+    get_k.wait()
+    own_ref[:, :rows] = jnp.transpose(k_ref[...].astype(jnp.float32)).astype(jnp.bfloat16)
+    get_v.wait()
+    puts = [pltpu.make_async_copy(own_ref, send_ref.at[c], out_sem.at[c]) for c in range(chips)]
+    for put in puts:
+        put.start()
+    for put in puts:
+        put.wait()
+
+
+def own_kernel(at_ref, doc_ref, q_ref, kv_ref, fq_ref, fk_ref, lhs_ref, sd_ref, peak_ref, phi_ref, nd_ref, v_own_ref):
     heads, hd, _ = fq_ref.shape
     rows = q_ref.shape[0]
     anchor = (2 * at_ref[0] + at_ref[1]) * rows
     q_pos = anchor + lax.broadcasted_iota(jnp.int32, (rows, 1), 0)
     k_pos = anchor + lax.broadcasted_iota(jnp.int32, (1, rows), 1)
     mask = (k_pos >= doc_start(doc_ref, q_pos)) & (k_pos <= q_pos)
-    k = k_ref[...]
-    v = with_ones(v_ref[...])
+    k_t = kv_ref[:, :rows]
+    v = with_ones(kv_ref[:, rows:])
     v_own_ref[...] = v
     for h in range(heads):
         q = q_ref[:, h * hd:(h + 1) * hd]
         lhs_ref[h * rows:(h + 1) * rows, :] = q
         fk_t = jnp.transpose(fk_ref[h].astype(jnp.float32)).astype(jnp.bfloat16)
         lhs_ref[heads * rows + h * hd:heads * rows + (h + 1) * hd, :] = fk_t
-        sd_ref[h] = jnp.where(mask, dot(q, k, NT) * (hd ** -0.5 * LOG2E), NEG)
+        sd = jnp.where(mask, dot(q, k_t) * (hd ** -0.5 * LOG2E), NEG)
+        sd_ref[h] = sd
+        peak_ref[h] = jnp.broadcast_to(jnp.max(sd, axis=1, keepdims=True), sd.shape)
         phi_q = softmaxes(dot(q, fq_ref[h]), 1)
         phi_ref[h] = phi_q
-        phi_k = softmaxes(dot(fk_t, k, NT), 0)
+        phi_k = softmaxes(dot(fk_t, k_t), 0)
         affinity = jnp.where(mask, dot(phi_q, phi_k), 0.0)
         nd_ref[h] = split_dot(affinity, v)
 
@@ -94,7 +109,7 @@
 
     for i in range(s_ref.shape[0]):
         c = c0 + 2 * i
-        low, high = jnp.maximum(c, 0), jnp.maximum(c + 1, 0)
+        low, high = slot(c, kv_ref.shape[0]), slot(c + 1, kv_ref.shape[0])
         k_t = jnp.concatenate([kv_ref[low, :, :hd], kv_ref[high, :, :hd]], axis=1)
         v = jnp.concatenate([kv_ref[low, :, hd:], kv_ref[high, :, hd:]], axis=0)
         z = dot(lhs_ref[...], k_t)
@@ -125,7 +140,7 @@
 
 
 def other_core_kernel(
-    at_ref, doc_ref, a_ref, b_ref, lhs_ref, sa_ref, max_a_ref, state_a_ref, sd_ref, phi_ref, nd_ref, v_own_ref,
+    at_ref, doc_ref, a_ref, b_ref, lhs_ref, sa_ref, max_a_ref, state_a_ref, sd_ref, peak_ref, phi_ref, nd_ref, v_own_ref,
     res_ref, loss_ref, sb_ref, max_ref, state_ref, acc_ref,
 ):
     heads, rows, hd = sd_ref.shape
@@ -142,9 +157,7 @@
         at = slice(h * rows, (h + 1) * rows)
         sd = sd_ref[h]
         off = jnp.broadcast_to(jnp.max(max_ref[at], axis=1, keepdims=True), (rows, hd))
-        peak = jnp.maximum(
-            jnp.broadcast_to(jnp.max(sd, axis=1, keepdims=True), (rows, hd)), jnp.where(carried, off, NEG)
-        )
+        peak = jnp.maximum(peak_ref[h], jnp.where(carried, off, NEG))
         acc_ref[at] = dot(jnp.exp2(sd - peak).astype(jnp.bfloat16), v_own_ref[...])
         max_ref[at] = jnp.where(carried, peak, -NEG)
 
@@ -152,7 +165,7 @@
     for kv_ref, s_ref, c0 in ((a_ref, sa_ref, a0), (b_ref, sb_ref, b0)):
         for i in range(steps):
             c = c0 + 2 * i
-            low, high = jnp.maximum(c, 0), jnp.maximum(c + 1, 0)
+            low, high = slot(c, kv_ref.shape[0]), slot(c + 1, kv_ref.shape[0])
             peak = max_ref[...]
             s = s_ref[i]
             weights.append(jnp.exp2(s[:, :rows] - peak).astype(jnp.bfloat16))
@@ -182,6 +195,13 @@
 F32, BF16 = jnp.float32, jnp.bfloat16
 SMEM = pl.BlockSpec(memory_space=pltpu.SMEM)
 VMEM = pl.BlockSpec(memory_space=pltpu.VMEM)
+HBM = pl.BlockSpec(memory_space=pltpu.HBM)
+
+
+def rotated(array, axis, first):
+    size = lax.axis_size(axis)
+    group = [(first + j) % size for j in range(size)]
+    return lax.all_to_all(array, axis, 0, 0, tiled=True, axis_index_groups=[group])
 
 
 def shapes(*items):
@@ -192,19 +212,23 @@
     return pltpu.CompilerParams(vmem_limit_bytes=mib * 1024 * 1024)
 
 
-def to_send(k_own, v_own, chips):
-    rows, hd = k_own.shape
+def to_send(keys, values, chips, hd):
+    rows = keys.shape[0]
     return pl.pallas_call(
         send_kernel,
-        out_shape=jax.ShapeDtypeStruct((chips, hd, rows + hd), BF16),
-        in_specs=[VMEM, VMEM],
-        out_specs=VMEM,
-        compiler_params=params(8),
+        out_shape=shapes(((chips, hd, rows + hd), BF16), ((hd, rows + hd), BF16)),
+        in_specs=[HBM, HBM],
+        out_specs=(HBM, VMEM),
+        scratch_shapes=[
+            pltpu.VMEM((rows, hd), BF16),
+            pltpu.SemaphoreType.DMA((2,)),
+            pltpu.SemaphoreType.DMA((chips,)),
+        ],
         name="to_send",
-    )(k_own, v_own)
-
-
-def own_block(at, doc_lengths, queries, k_own, v_own, fq_weight, fk_weight):
+    )(keys, values)
+
+
+def own_block(at, doc_lengths, queries, kv_own, fq_weight, fk_weight):
     rows = queries.shape[0]
     heads, hd, _ = fq_weight.shape
     return pl.pallas_call(
@@ -212,16 +236,17 @@
         out_shape=shapes(
             ((heads * (rows + hd), hd), BF16),
             ((heads, rows, rows), F32),
+            ((heads, rows, rows), F32),
             ((heads, rows, 2 * hd), BF16),
             ((heads, rows, 2 * hd), F32),
             ((rows, 2 * hd), BF16),
         ),
-        in_specs=[SMEM, SMEM] + [VMEM] * 5,
-        out_specs=(VMEM,) * 5,
+        in_specs=[SMEM, SMEM] + [VMEM] * 4,
+        out_specs=(VMEM,) * 6,
         compiler_params=params(16),
         cost_estimate=pl.CostEstimate(flops=10**9, bytes_accessed=2 * 10**6, transcendentals=10**6),
         name="own_block",
-    )(at, doc_lengths, queries, k_own, v_own, fq_weight, fk_weight)
+    )(at, doc_lengths, queries, kv_own, fq_weight, fk_weight)
 
 
 def same_core(at, doc_lengths, a, lhs, heads):
@@ -240,12 +265,12 @@
     )(at, doc_lengths, a, lhs)
 
 
-def other_core(at, doc_lengths, a, b, lhs, sa, max_a, state_a, sd, phi, nd, v_own, planes):
+def other_core(at, doc_lengths, a, b, lhs, sa, max_a, state_a, sd, peak, phi, nd, v_own, planes):
     heads, rows, hd = sd.shape
     return pl.pallas_call(
         other_core_kernel,
         out_shape=shapes(((rows, heads * hd), F32), ((planes, rows), F32)),
-        in_specs=[SMEM, SMEM] + [VMEM] * 10,
+        in_specs=[SMEM, SMEM] + [VMEM] * 11,
         out_specs=(VMEM, VMEM),
         scratch_shapes=[
             pltpu.VMEM(sa.shape, F32),
@@ -256,25 +281,22 @@
         compiler_params=params(24),
         cost_estimate=pl.CostEstimate(flops=4 * 10**9, bytes_accessed=4 * 10**6, transcendentals=4 * 10**6),
         name="other_core",
-    )(at, doc_lengths, a, b, lhs, sa, max_a, state_a, sd, phi, nd, v_own)
+    )(at, doc_lengths, a, b, lhs, sa, max_a, state_a, sd, peak, phi, nd, v_own)
 
 
 def body(queries, keys, values, doc_lengths, fq_weight, fk_weight):
     heads, hd, _ = fq_weight.shape
-    kv_head = lax.axis_index("head") * heads // (QH // KVH)
     at = jnp.stack([lax.axis_index(CHIP), lax.axis_index(CORE)]).astype(jnp.int32)
-    k_own = lax.dynamic_slice_in_dim(keys, kv_head * hd, hd, 1)
-    v_own = lax.dynamic_slice_in_dim(values, kv_head * hd, hd, 1)
-    send = to_send(k_own, v_own, lax.axis_size(CHIP))
-    a = lax.all_to_all(send, CHIP, 0, 0, tiled=True)
-    lhs, sd, phi, nd, v_own = own_block(at, doc_lengths, queries, k_own, v_own, fq_weight, fk_weight)
+    send, kv_own = to_send(keys, values, lax.axis_size(CHIP), hd)
+    a = rotated(send, CHIP, FIRST_CHIP)
+    lhs, sd, peak, phi, nd, v_own = own_block(at, doc_lengths, queries, kv_own, fq_weight, fk_weight)
     a, lhs = lax.optimization_barrier((a, lhs))
     b = lax.ppermute(a, CORE, [(0, 1), (1, 0)])
     sa, max_a, state_a = same_core(at, doc_lengths, a, lhs, heads)
     residual, loss = other_core(
-        at, doc_lengths, a, b, lhs, sa, max_a, state_a, sd, phi, nd, v_own, lax.axis_size("head")
+        at, doc_lengths, a, b, lhs, sa, max_a, state_a, sd, peak, phi, nd, v_own, lax.axis_size("head")
     )
-    parts = lax.all_to_all(loss, "head", 0, 0, tiled=True)
+    parts = rotated(loss, "head", FIRST_PLANE)
     return residual, jnp.sum(parts, axis=0)
 
 

time: 64.7 us -> 56.9 us (0.88)
  the two profiles are of different devices: /device:TPU:1 before, /device:TPU:24 now
where the time goes in v3:
time: 56.9 us; the launch traced here: 56.5 us
  blocking collectives  21.4 us (38%)
  starting transfers between devices  12.2 us (21%)
  Pallas kernels  12 us (21%)
  waiting for transfers between devices  9.43 us (17%)
  between operations  0.72 us (1%)
  other arithmetic  0.62 us (1%)
    all_to_all x1, blocking collectives, rotated(): lax.all_to_all(array, axis, 0, 0, tiled=True, axis_index_groups=[group])  21.4 us
    all_to_all x1, starting transfers between devices, rotated(): lax.all_to_all(array, axis, 0, 0, tiled=True, axis_index_groups=[group])  10.3 us
    all_to_all x1, waiting for transfers between devices, rotated(): lax.all_to_all(array, axis, 0, 0, tiled=True, axis_index_groups=[group])  9.39 us
    pallas_call x1, Pallas kernels, other_core(): pl.pallas_call(other_core_kernel, out_shape=shapes(((rows, heads * hd), F...  4.47 us
    pallas_call x1, Pallas kernels, to_send(): pl.pallas_call(send_kernel, out_shape=shapes(((chips, hd, rows + hd), BF1...  2.69 us
    pallas_call x1, Pallas kernels, same_core(): pl.pallas_call(same_core_kernel, out_shape=shapes(((steps, heads * rows,...  2.58 us
    pallas_call x1, Pallas kernels, own_block(): pl.pallas_call(own_kernel, out_shape=shapes(((heads * (rows + hd), hd), B...  2.29 us
    ppermute x1, starting transfers between devices, body(): b = lax.ppermute(a, CORE, [(0, 1), (1, 0)])  1.91 us
  transfers between devices with their start and end apart: 2, of which 1 were waited for; matrix products, arithmetic and copies ran while one was open for 0% of the time, Pallas kernels for 9%

profile of v3, /device:TPU:24, one launch (start us, length us, event | category | flops | bytes accessed | tf_op | source)
XLA Modules:
  0.0 56.5 jit_solution(15806059903321271983)
XLA Ops:
  0.6 0.0 copy-start.4
  0.6 0.0 copy-start.2
  0.7 0.0 copy-start.1
  0.7 0.0 copy-start
  0.7 2.7 %to_send.1 = (bf16[16,128,256]{2,1,0:T(8,128)(2,1)}, bf16[128,256]{1,0:T(8,128)(2,1)}) custom-call(bf16[128,1024]{1,0:T(8,128)(2,1)} %keys_ref.1, bf16[128,1024]{1,0:T(8,128)(2,1)} %values_ref.1), custom_call_target="tpu_custom_call" | custom-call | tf_op jit(solution)/shard_map/to_send/pallas_call | solution.py:217
  3.4 0.0 copy-start.3
  3.4 10.3 %all-to-all-start = ((bf16[16,128,256]{2,1,0:T(8,128)(2,1)}), bf16[16,128,256]{2,1,0:T(8,128)(2,1)S(1)}, u32[]{:S(2)}, u32[]{:S(2)}) async-start(bf16[16,128,256]{2,1,0:T(8,128)(2,1)} %get-tuple-element.17), calls=%async_computation | async-start | bytes 2097152 | tf_op jit(solution)/shard_map/all_to_all | solution.py:204
  13.7 0.1 pad_add_fusion.at_ref
  13.8 0.0 copy-done.4
  13.8 0.0 copy-done.2
  13.8 0.0 copy-done.1
  13.8 0.0 copy-done
  13.8 0.0 copy-done.3
  13.8 2.3 %own_block.1 = (bf16[1024,128]{1,0:T(8,128)(2,1)S(1)}, f32[4,128,128]{2,1,0:T(8,128)S(1)}, f32[4,128,128]{2,1,0:T(8,128)S(1)}, bf16[4,128,256]{2,1,0:T(8,128)(2,...) custom-call(s32[2]{0:T(128)S(1)} %pad_add_fusion.at_ref, s32[12]{0:T(128)S(1)} %copy-done.4, ...), custom_call_target="tpu_custom_call" | custom-call | flops 1000000000 | bytes 2000000 | tf_op jit(solution)/shard_map/own_block/pallas_call | solution.py:234
  16.1 9.4 %all-to-all-done.a_ref = bf16[16,128,256]{2,1,0:T(8,128)(2,1)S(1)} async-done(((bf16[16,128,256]{2,1,0:T(8,128)(2,1)}), bf16[16,128,256]{2,1,0:T(8,128)(2,1)S(1)}, u32[]{:S(2)}, u32[]{:S(2)}) %all-to-all-start) | async-done | bytes 1048608 | tf_op jit(solution)/shard_map/all_to_all | solution.py:204
  25.5 1.9 %collective-permute-start = (bf16[16,128,256]{2,1,0:T(8,128)(2,1)S(1)}, bf16[16,128,256]{2,1,0:T(8,128)(2,1)S(1)}, u32[]{:S(2)}, u32[]{:S(2)}) collective-permute-start(bf16[16,128,256]{2,1,0:T(8,128)(2,1)S(1)} %all-to-all-done.a_ref), channel_id=1, source_target_pairs={{0,16},{16,0},{1,17},{17,1},{2,18},{18,2},{3,19},{19,3},{4,20},{20... | collective-permute-start | bytes 3145736 | tf_op jit(solution)/shard_map/ppermute | solution.py:294
  27.4 2.6 %same_core.1 = (f32[4,512,256]{2,1,0:T(8,128)S(1)}, f32[512,128]{1,0:T(8,128)S(1)}, f32[4,256,256]{2,1,0:T(8,128)S(1)}) custom-call(s32[2]{0:T(128)S(1)} %pad_add_fusion.at_ref, s32[12]{0:T(128)S(1)} %copy-done.4, bf16[16,128,256]{2,1,0:T(8,128)(2,1)S(1)} %all-to-all-done.a_ref, bf16[1024,128]{1,0:T(8,128)(2,1)S(1)} %get-tuple-element.21.lhs_ref), custom_call_target="tpu_custom_call" | custom-call | flops 2000000000 | bytes 4000000 | tf_op jit(solution)/shard_map/same_core/pallas_call | solution.py:255
  30.0 0.0 collective-permute-done.b_ref
  30.0 4.5 %other_core.1 = (f32[128,512]{1,0:T(8,128)}, f32[16,128]{1,0:T(8,128)S(1)}) custom-call(s32[2]{0:T(128)S(1)} %pad_add_fusion.at_ref, s32[12]{0:T(128)S(1)} %copy-done.4, bf16[16,128,256]{2,1,0:T(8,128)(2,1)S(1)} %all-to-all-done.a_ref, bf16[16,128,256]{2,1,0:T(8,128)(2,1)S(1)} %collective-permute-done.b_ref, ...), custom_call_target="tpu_custom_call" | custom-call | flops 4000000000 | bytes 4000000 | tf_op jit(solution)/shard_map/other_core/pallas_call | solution.py:270
  34.5 21.4 %all_to_all.14 = f32[16,1,128]{2,1,0:T(1,128)S(1)} all-to-all(f32[16,1,128]{2,1,0:T(1,128)S(1)} %bitcast.5), channel_id=1, replica_groups={{8,9,10,11,12,13,14,15,0,1,2,3,4,5,6,7},{24,25,26,27,28,29,30,31,16,17,..., dimensions={0} | all-to-all | bytes 16384 | tf_op jit(solution)/shard_map/all_to_all | solution.py:204
  55.9 0.5 reduce_sum.9
Async XLA Ops:
  0.6 13.1 %copy-start.4 = (s32[12]{0:T(128)S(1)}, s32[12]{0:T(128)}, u32[]{:S(2)}) copy-start(s32[12]{0:T(128)} %doc_ref.5) | copy-start | bytes 148
  0.6 13.1 %copy-start.2 = (bf16[4,128,128]{2,1,0:T(8,128)(2,1)S(1)}, bf16[4,128,128]{2,1,0:T(8,128)(2,1)}, u32[]{:S(2)}) copy-start(bf16[4,128,128]{2,1,0:T(8,128)(2,1)} %fk_ref.1) | copy-start | bytes 393220
  0.7 13.1 %copy-start.1 = (bf16[4,128,128]{2,1,0:T(8,128)(2,1)S(1)}, bf16[4,128,128]{2,1,0:T(8,128)(2,1)}, u32[]{:S(2)}) copy-start(bf16[4,128,128]{2,1,0:T(8,128)(2,1)} %fq_ref.1) | copy-start | bytes 393220
  0.7 13.1 %copy-start = (bf16[128,512]{1,0:T(8,128)(2,1)S(1)}, bf16[128,512]{1,0:T(8,128)(2,1)}, u32[]{:S(2)}) copy-start(bf16[128,512]{1,0:T(8,128)(2,1)} %q_ref.1) | copy-start | bytes 393220
  3.4 10.4 %copy-start.3 = (bf16[128,256]{1,0:T(8,128)(2,1)S(1)}, bf16[128,256]{1,0:T(8,128)(2,1)}, u32[]{:S(2)}) copy-start(bf16[128,256]{1,0:T(8,128)(2,1)} %get-tuple-element.18.kv_ref) | copy-start | bytes 196612
  3.4 22.1 %all-to-all-start = ((bf16[16,128,256]{2,1,0:T(8,128)(2,1)}), bf16[16,128,256]{2,1,0:T(8,128)(2,1)S(1)}, u32[]{:S(2)}, u32[]{:S(2)}) async-start(bf16[16,128,256]{2,1,0:T(8,128)(2,1)} %get-tuple-element.17), calls=%async_computation | async-start | bytes 2097152 | tf_op jit(solution)/shard_map/all_to_all | solution.py:204
  25.5 4.5 %collective-permute-start = (bf16[16,128,256]{2,1,0:T(8,128)(2,1)S(1)}, bf16[16,128,256]{2,1,0:T(8,128)(2,1)S(1)}, u32[]{:S(2)}, u32[]{:S(2)}) collective-permute-start(bf16[16,128,256]{2,1,0:T(8,128)(2,1)S(1)} %all-to-all-done.a_ref), channel_id=1, source_target_pairs={{0,16},{16,0},{1,17},{17,1},{2,18},{18,2},{3,19},{19,3},{4,20},{20... | collective-permute-start | bytes 3145736 | tf_op jit(solution)/shard_map/ppermute | solution.py:294

commit v4 on v3

--- a/solution.py
+++ b/solution.py
@@ -13,7 +13,7 @@
 CORE = "seq_2"
 SEQ = (*CHIP, CORE)
 NEG = -1e30
-FIRST_CHIP, FIRST_PLANE = 10, 8
+FIRST_CHIP, FIRST_PLANE = 14, 10
 LOG2E = math.log2(math.e)
 
 
@@ -51,25 +51,6 @@
 
 def with_ones(v):
     return jnp.concatenate([v, jnp.ones_like(v)], axis=1)
-
-
-def send_kernel(keys_ref, values_ref, send_ref, own_ref, k_ref, in_sem, out_sem):
-    chips, hd, _ = send_ref.shape
-    rows = k_ref.shape[0]
-    column = lax.axis_index("head") * keys_ref.shape[1] // (hd * lax.axis_size("head"))
-    at = pl.ds(pl.multiple_of(column * hd, hd), hd)
-    get_k = pltpu.make_async_copy(keys_ref.at[:, at], k_ref, in_sem.at[0])
-    get_v = pltpu.make_async_copy(values_ref.at[:, at], own_ref.at[:, pl.ds(rows, hd)], in_sem.at[1])
-    get_k.start()
-    get_v.start()
-    get_k.wait()
-    own_ref[:, :rows] = jnp.transpose(k_ref[...].astype(jnp.float32)).astype(jnp.bfloat16)
-    get_v.wait()
-    puts = [pltpu.make_async_copy(own_ref, send_ref.at[c], out_sem.at[c]) for c in range(chips)]
-    for put in puts:
-        put.start()
-    for put in puts:
-        put.wait()
 
 
 def own_kernel(at_ref, doc_ref, q_ref, kv_ref, fq_ref, fk_ref, lhs_ref, sd_ref, peak_ref, phi_ref, nd_ref, v_own_ref):
@@ -195,7 +176,6 @@
 F32, BF16 = jnp.float32, jnp.bfloat16
 SMEM = pl.BlockSpec(memory_space=pltpu.SMEM)
 VMEM = pl.BlockSpec(memory_space=pltpu.VMEM)
-HBM = pl.BlockSpec(memory_space=pltpu.HBM)
 
 
 def rotated(array, axis, first):
@@ -210,22 +190,6 @@
 
 def params(mib):
     return pltpu.CompilerParams(vmem_limit_bytes=mib * 1024 * 1024)
-
-
-def to_send(keys, values, chips, hd):
-    rows = keys.shape[0]
-    return pl.pallas_call(
-        send_kernel,
-        out_shape=shapes(((chips, hd, rows + hd), BF16), ((hd, rows + hd), BF16)),
-        in_specs=[HBM, HBM],
-        out_specs=(HBM, VMEM),
-        scratch_shapes=[
-            pltpu.VMEM((rows, hd), BF16),
-            pltpu.SemaphoreType.DMA((2,)),
-            pltpu.SemaphoreType.DMA((chips,)),
-        ],
-        name="to_send",
-    )(keys, values)
 
 
 def own_block(at, doc_lengths, queries, kv_own, fq_weight, fk_weight):
@@ -287,7 +251,11 @@
 def body(queries, keys, values, doc_lengths, fq_weight, fk_weight):
     heads, hd, _ = fq_weight.shape
     at = jnp.stack([lax.axis_index(CHIP), lax.axis_index(CORE)]).astype(jnp.int32)
-    send, kv_own = to_send(keys, values, lax.axis_size(CHIP), hd)
+    kv_head = lax.axis_index("head") * (keys.shape[1] // hd) // lax.axis_size("head")
+    k_own = lax.dynamic_slice_in_dim(keys, kv_head * hd, hd, 1)
+    v_own = lax.dynamic_slice_in_dim(values, kv_head * hd, hd, 1)
+    kv_own = jnp.concatenate([k_own.T, v_own], axis=1)
+    send = jnp.broadcast_to(kv_own, (lax.axis_size(CHIP), *kv_own.shape))
     a = rotated(send, CHIP, FIRST_CHIP)
     lhs, sd, peak, phi, nd, v_own = own_block(at, doc_lengths, queries, kv_own, fq_weight, fk_weight)
     a, lhs = lax.optimization_barrier((a, lhs))

time: 56.9 us -> 55.6 us (0.977)
  Pallas kernels: 12 us -> 9.27 us
  local copies, waits for them, and re-layouts: 0.02 us -> 2.06 us
    pallas_call x1 -> x0, Pallas kernels: 2.69 us -> none  [to_send(): pl.pallas_call(send_kernel, out_shape=shapes(((chips, hd, rows + hd), BF1...]
    broadcast_in_dim x0 -> x1, local copies, waits for them, and re-layouts: none -> 1.07 us  [body(): send = jnp.broadcast_to(kv_own, (lax.axis_size(CHIP), *kv_own.shape))]
    dynamic_slice x0 -> x1, local copies, waits for them, and re-layouts: none -> 0.87 us  [body(): v_own = lax.dynamic_slice_in_dim(values, kv_head * hd, hd, 1)]
  transfers between devices with their start and end apart: 2 -> 2, of which waited for: 1 -> 2; matrix products, arithmetic and copies ran while one was open for 0% -> 0% of each run, Pallas kernels for 9% -> 9%
where the time goes in v4:
time: 55.6 us; the launch traced here: 55.4 us
  blocking collectives  21 us (38%)
  starting transfers between devices  11.8 us (21%)
  waiting for transfers between devices  9.88 us (18%)
  Pallas kernels  9.27 us (17%)
  local copies, waits for them, and re-layouts  2.06 us (4%)
  between operations  0.73 us (1%)
  other arithmetic  0.63 us (1%)
    all_to_all x1, blocking collectives, rotated(): lax.all_to_all(array, axis, 0, 0, tiled=True, axis_index_groups=[group])  21 us
    all_to_all x1, starting transfers between devices, rotated(): lax.all_to_all(array, axis, 0, 0, tiled=True, axis_index_groups=[group])  9.85 us
    all_to_all x1, waiting for transfers between devices, rotated(): lax.all_to_all(array, axis, 0, 0, tiled=True, axis_index_groups=[group])  9.82 us
    pallas_call x1, Pallas kernels, other_core(): pl.pallas_call(other_core_kernel, out_shape=shapes(((rows, heads * hd), F...  4.42 us
    pallas_call x1, Pallas kernels, same_core(): pl.pallas_call(same_core_kernel, out_shape=shapes(((steps, heads * rows,...  2.57 us
    pallas_call x1, Pallas kernels, own_block(): pl.pallas_call(own_kernel, out_shape=shapes(((heads * (rows + hd), hd), B...  2.29 us
    ppermute x1, starting transfers between devices, body(): b = lax.ppermute(a, CORE, [(0, 1), (1, 0)])  1.91 us
  transfers between devices with their start and end apart: 2, of which 2 were waited for; matrix products, arithmetic and copies ran while one was open for 0% of the time, Pallas kernels for 9%

profile of v4, /device:TPU:24, one launch (start us, length us, event | category | flops | bytes accessed | tf_op | source)
XLA Modules:
  0.0 55.4 jit_solution(1815891621993964876)
XLA Ops:
  0.6 0.0 copy-start.3
  0.6 0.0 copy-start.2
  0.7 0.0 copy-start.1
  0.7 0.0 copy-start
  0.7 0.9 %constant_dynamic-slice_fusion = (bf16[128,128]{1,0:T(8,128)(2,1)S(1)}, bf16[128,128]{1,0:T(8,128)(2,1)S(1)}) fusion(bf16[128,1024]{1,0:T(8,128)(2,1)} %param.8, s32[]{:T(128)S(6)} %select_n.10, bf16[128,1024]{1,0:T(8,128)(2,1)} %param.7), kind=kLoop, calls=%fused_computation.2 | loop fusion | bytes 131076 | tf_op jit(solution)/shard_map/dynamic_slice | solution.py:256
  1.6 0.1 copy.11
  1.7 1.1 %broadcast_in_dim.3 = bf16[16,128,256]{2,1,0:T(8,128)(2,1)} broadcast(bf16[128,256]{1,0:T(8,128)(2,1)S(1)} %pad_maximum_fusion.kv_ref), dimensions={1,2} | broadcast | bytes 1114112 | tf_op jit(solution)/shard_map/broadcast_in_dim | solution.py:258
  2.8 9.9 %all-to-all-start = ((bf16[16,128,256]{2,1,0:T(8,128)(2,1)}), bf16[16,128,256]{2,1,0:T(8,128)(2,1)S(1)}, u32[]{:S(2)}, u32[]{:S(2)}) async-start(bf16[16,128,256]{2,1,0:T(8,128)(2,1)} %broadcast_in_dim.3), calls=%async_computation | async-start | bytes 2097152 | tf_op jit(solution)/shard_map/all_to_all | solution.py:184
  12.6 0.1 pad_add_fusion.at_ref
  12.7 0.0 copy-done.3
  12.7 0.0 copy-done.2
  12.7 0.0 copy-done.1
  12.7 0.0 copy-done
  12.7 2.3 %own_block.1 = (bf16[1024,128]{1,0:T(8,128)(2,1)S(1)}, f32[4,128,128]{2,1,0:T(8,128)S(1)}, f32[4,128,128]{2,1,0:T(8,128)S(1)}, bf16[4,128,256]{2,1,0:T(8,128)(2,...) custom-call(s32[2]{0:T(128)S(1)} %pad_add_fusion.at_ref, s32[12]{0:T(128)S(1)} %copy-done.3, ...), custom_call_target="tpu_custom_call" | custom-call | flops 1000000000 | bytes 2000000 | tf_op jit(solution)/shard_map/own_block/pallas_call | solution.py:198
  15.0 9.8 %all-to-all-done.a_ref = bf16[16,128,256]{2,1,0:T(8,128)(2,1)S(1)} async-done(((bf16[16,128,256]{2,1,0:T(8,128)(2,1)}), bf16[16,128,256]{2,1,0:T(8,128)(2,1)S(1)}, u32[]{:S(2)}, u32[]{:S(2)}) %all-to-all-start) | async-done | bytes 1048608 | tf_op jit(solution)/shard_map/all_to_all | solution.py:184
  24.8 1.9 %collective-permute-start = (bf16[16,128,256]{2,1,0:T(8,128)(2,1)S(1)}, bf16[16,128,256]{2,1,0:T(8,128)(2,1)S(1)}, u32[]{:S(2)}, u32[]{:S(2)}) collective-permute-start(bf16[16,128,256]{2,1,0:T(8,128)(2,1)S(1)} %all-to-all-done.a_ref), channel_id=1, source_target_pairs={{0,16},{16,0},{1,17},{17,1},{2,18},{18,2},{3,19},{19,3},{4,20},{20... | collective-permute-start | bytes 3145736 | tf_op jit(solution)/shard_map/ppermute | solution.py:262
  26.7 2.6 %same_core.1 = (f32[4,512,256]{2,1,0:T(8,128)S(1)}, f32[512,128]{1,0:T(8,128)S(1)}, f32[4,256,256]{2,1,0:T(8,128)S(1)}) custom-call(s32[2]{0:T(128)S(1)} %pad_add_fusion.at_ref, s32[12]{0:T(128)S(1)} %copy-done.3, bf16[16,128,256]{2,1,0:T(8,128)(2,1)S(1)} %all-to-all-done.a_ref, bf16[1024,128]{1,0:T(8,128)(2,1)S(1)} %get-tuple-element.17.lhs_ref), custom_call_target="tpu_custom_call" | custom-call | flops 2000000000 | bytes 4000000 | tf_op jit(solution)/shard_map/same_core/pallas_call | solution.py:219
  29.3 0.1 collective-permute-done.b_ref
  29.4 4.4 %other_core.1 = (f32[128,512]{1,0:T(8,128)}, f32[16,128]{1,0:T(8,128)S(1)}) custom-call(s32[2]{0:T(128)S(1)} %pad_add_fusion.at_ref, s32[12]{0:T(128)S(1)} %copy-done.3, bf16[16,128,256]{2,1,0:T(8,128)(2,1)S(1)} %all-to-all-done.a_ref, bf16[16,128,256]{2,1,0:T(8,128)(2,1)S(1)} %collective-permute-done.b_ref, ...), custom_call_target="tpu_custom_call" | custom-call | flops 4000000000 | bytes 4000000 | tf_op jit(solution)/shard_map/other_core/pallas_call | solution.py:234
  33.8 21.0 %all_to_all.14 = f32[16,1,128]{2,1,0:T(1,128)S(1)} all-to-all(f32[16,1,128]{2,1,0:T(1,128)S(1)} %bitcast.6), channel_id=1, replica_groups={{10,11,12,13,14,15,0,1,2,3,4,5,6,7,8,9},{26,27,28,29,30,31,16,17,18,19,..., dimensions={0} | all-to-all | bytes 16384 | tf_op jit(solution)/shard_map/all_to_all | solution.py:184
  54.8 0.5 reduce_sum.9
  (1 shorter events, 0.0 us)
Async XLA Ops:
  0.6 12.1 %copy-start.3 = (s32[12]{0:T(128)S(1)}, s32[12]{0:T(128)}, u32[]{:S(2)}) copy-start(s32[12]{0:T(128)} %doc_ref.5) | copy-start | bytes 148
  0.6 12.1 %copy-start.2 = (bf16[4,128,128]{2,1,0:T(8,128)(2,1)S(1)}, bf16[4,128,128]{2,1,0:T(8,128)(2,1)}, u32[]{:S(2)}) copy-start(bf16[4,128,128]{2,1,0:T(8,128)(2,1)} %fk_ref.1) | copy-start | bytes 393220
  0.7 12.1 %copy-start.1 = (bf16[4,128,128]{2,1,0:T(8,128)(2,1)S(1)}, bf16[4,128,128]{2,1,0:T(8,128)(2,1)}, u32[]{:S(2)}) copy-start(bf16[4,128,128]{2,1,0:T(8,128)(2,1)} %fq_ref.1) | copy-start | bytes 393220
  0.7 12.0 %copy-start = (bf16[128,512]{1,0:T(8,128)(2,1)S(1)}, bf16[128,512]{1,0:T(8,128)(2,1)}, u32[]{:S(2)}) copy-start(bf16[128,512]{1,0:T(8,128)(2,1)} %q_ref.1) | copy-start | bytes 393220
  2.8 22.1 %all-to-all-start = ((bf16[16,128,256]{2,1,0:T(8,128)(2,1)}), bf16[16,128,256]{2,1,0:T(8,128)(2,1)S(1)}, u32[]{:S(2)}, u32[]{:S(2)}) async-start(bf16[16,128,256]{2,1,0:T(8,128)(2,1)} %broadcast_in_dim.3), calls=%async_computation | async-start | bytes 2097152 | tf_op jit(solution)/shard_map/all_to_all | solution.py:184
  24.8 4.5 %collective-permute-start = (bf16[16,128,256]{2,1,0:T(8,128)(2,1)S(1)}, bf16[16,128,256]{2,1,0:T(8,128)(2,1)S(1)}, u32[]{:S(2)}, u32[]{:S(2)}) collective-permute-start(bf16[16,128,256]{2,1,0:T(8,128)(2,1)S(1)} %all-to-all-done.a_ref), channel_id=1, source_target_pairs={{0,16},{16,0},{1,17},{17,1},{2,18},{18,2},{3,19},{19,3},{4,20},{20... | collective-permute-start | bytes 3145736 | tf_op jit(solution)/shard_map/ppermute | solution.py:262

commit v5 on v4

--- a/solution.py
+++ b/solution.py
@@ -1,3 +1,4 @@
+import functools
 import math
 
 import jax
@@ -78,7 +79,7 @@
         nd_ref[h] = split_dot(affinity, v)
 
 
-def scan_keys(kv_ref, lhs_ref, s_ref, max_ref, state_ref, c0, parity, first, anchor, before):
+def scan_keys(kv_ref, lhs_ref, s_ref, max_ref, state_ref, c0, parity, first, anchor, before, skip):
     heads, rows, hd = state_ref.shape[0], max_ref.shape[1], kv_ref.shape[1]
     qr = heads * rows
     scale = hd ** -0.5 * LOG2E
@@ -88,7 +89,7 @@
         pos = (2 * c + parity) * rows + lane + jnp.where(lane < rows, 0, rows)
         return (pos >= first) & (pos < anchor)
 
-    for i in range(s_ref.shape[0]):
+    for i in range(skip, s_ref.shape[0]):
         c = c0 + 2 * i
         low, high = slot(c, kv_ref.shape[0]), slot(c + 1, kv_ref.shape[0])
         k_t = jnp.concatenate([kv_ref[low, :, :hd], kv_ref[high, :, :hd]], axis=1)
@@ -97,7 +98,7 @@
         s = jnp.where(visible(c, (1, 2 * rows), 1), z[:qr] * scale, NEG)
         s_ref[i] = s
         m = jnp.maximum(s[:, :rows], s[:, rows:])
-        if i > 0:
+        if i > skip:
             m = jnp.maximum(max_ref[...], m)
         elif before is not None:
             m = jnp.maximum(before[0][...], m)
@@ -105,11 +106,20 @@
         v = with_ones(v) * jnp.where(visible(c, (2 * rows, 1), 0), 1.0, 0.0).astype(jnp.bfloat16)
         for h in range(heads):
             d = dot(softmaxes(z[qr + h * hd:qr + (h + 1) * hd], 0), v)
-            if i > 0:
+            if i > skip:
                 d = state_ref[h] + d
             elif before is not None:
                 d = before[1][h] + d
             state_ref[h] = d
+
+
+def as_far_as_needed(first, anchor, rows, steps, run):
+    skips = (steps - 1, steps // 2, 0)
+    nearer = False
+    for skip in skips:
+        reached = first >= anchor - 4 * (steps - skip) * rows if skip else True
+        pl.when(jnp.logical_and(reached, jnp.logical_not(nearer)))(functools.partial(run, skip))
+        nearer = jnp.logical_or(nearer, reached)
 
 
 def same_core_kernel(at_ref, doc_ref, a_ref, lhs_ref, s_ref, max_ref, state_ref):
@@ -117,7 +127,12 @@
     chip, core = at_ref[0], at_ref[1]
     anchor = (2 * chip + core) * rows
     first = doc_start(doc_ref, anchor)
-    scan_keys(a_ref, lhs_ref, s_ref, max_ref, state_ref, chip - 2 * s_ref.shape[0], core, first, anchor, None)
+    steps = s_ref.shape[0]
+
+    def run(skip):
+        scan_keys(a_ref, lhs_ref, s_ref, max_ref, state_ref, chip - 2 * steps, core, first, anchor, None, skip)
+
+    as_far_as_needed(first, anchor, rows, steps, run)
 
 
 def other_core_kernel(
@@ -130,30 +145,33 @@
     first = doc_start(doc_ref, anchor)
     steps = sb_ref.shape[0]
     a0, b0 = chip - 2 * steps, chip - 2 * steps + core
-    scan_keys(b_ref, lhs_ref, sb_ref, max_ref, state_ref, b0, 1 - core, first, anchor, (max_a_ref, state_a_ref))
-
     q_pos = anchor + lax.broadcasted_iota(jnp.int32, (rows, 1), 0)
     carried = jnp.broadcast_to(jnp.where(doc_start(doc_ref, q_pos) == first, 1.0, 0.0), (rows, hd)) > 0.5
-    for h in range(heads):
-        at = slice(h * rows, (h + 1) * rows)
-        sd = sd_ref[h]
-        off = jnp.broadcast_to(jnp.max(max_ref[at], axis=1, keepdims=True), (rows, hd))
-        peak = jnp.maximum(peak_ref[h], jnp.where(carried, off, NEG))
-        acc_ref[at] = dot(jnp.exp2(sd - peak).astype(jnp.bfloat16), v_own_ref[...])
-        max_ref[at] = jnp.where(carried, peak, -NEG)
-
-    weights, seen = [], []
-    for kv_ref, s_ref, c0 in ((a_ref, sa_ref, a0), (b_ref, sb_ref, b0)):
-        for i in range(steps):
-            c = c0 + 2 * i
-            low, high = slot(c, kv_ref.shape[0]), slot(c + 1, kv_ref.shape[0])
-            peak = max_ref[...]
-            s = s_ref[i]
-            weights.append(jnp.exp2(s[:, :rows] - peak).astype(jnp.bfloat16))
-            weights.append(jnp.exp2(s[:, rows:] - peak).astype(jnp.bfloat16))
-            seen.append(with_ones(kv_ref[low, :, hd:]))
-            seen.append(with_ones(kv_ref[high, :, hd:]))
-    acc_ref[...] += dot(jnp.concatenate(weights, axis=1), jnp.concatenate(seen, axis=0))
+
+    def run(skip):
+        before = (max_a_ref, state_a_ref)
+        scan_keys(b_ref, lhs_ref, sb_ref, max_ref, state_ref, b0, 1 - core, first, anchor, before, skip)
+        for h in range(heads):
+            at = slice(h * rows, (h + 1) * rows)
+            off = jnp.broadcast_to(jnp.max(max_ref[at], axis=1, keepdims=True), (rows, hd))
+            peak = jnp.maximum(peak_ref[h], jnp.where(carried, off, NEG))
+            acc_ref[at] = dot(jnp.exp2(sd_ref[h] - peak).astype(jnp.bfloat16), v_own_ref[...])
+            max_ref[at] = jnp.where(carried, peak, -NEG)
+
+        weights, seen = [], []
+        for kv_ref, s_ref, c0 in ((a_ref, sa_ref, a0), (b_ref, sb_ref, b0)):
+            for i in range(skip, steps):
+                c = c0 + 2 * i
+                low, high = slot(c, kv_ref.shape[0]), slot(c + 1, kv_ref.shape[0])
+                peak = max_ref[...]
+                s = s_ref[i]
+                weights.append(jnp.exp2(s[:, :rows] - peak).astype(jnp.bfloat16))
+                weights.append(jnp.exp2(s[:, rows:] - peak).astype(jnp.bfloat16))
+                seen.append(with_ones(kv_ref[low, :, hd:]))
+                seen.append(with_ones(kv_ref[high, :, hd:]))
+        acc_ref[...] += dot(jnp.concatenate(weights, axis=1), jnp.concatenate(seen, axis=0))
+
+    as_far_as_needed(first, anchor, rows, steps, run)
 
     squares = jnp.zeros((rows, hd), jnp.float32)
     for h in range(heads):

time: 55.6 us -> 54.5 us (0.980)
  Pallas kernels: 9.27 us -> 6.49 us
  waiting for transfers between devices: 9.88 us -> 11.1 us
    pallas_call x1, Pallas kernels: 4.42 us -> 2.82 us  [other_core(): pl.pallas_call(other_core_kernel, out_shape=shapes(((rows, heads * hd), F...]
    pallas_call x1, Pallas kernels: 2.57 us -> 1.39 us  [same_core(): pl.pallas_call(same_core_kernel, out_shape=shapes(((steps, heads * rows,...]
    ppermute x1, waiting for transfers between devices: 0.05 us -> 1.23 us  [body(): b = lax.ppermute(a, CORE, [(0, 1), (1, 0)])]
  transfers between devices with their start and end apart: 2 -> 2, of which waited for: 2 -> 2; matrix products, arithmetic and copies ran while one was open for 0% -> 0% of each run, Pallas kernels for 9% -> 7%
where the time goes in v5:
time: 54.5 us; the launch traced here: 53.8 us
  blocking collectives  21.1 us (39%)
  starting transfers between devices  11.8 us (22%)
  waiting for transfers between devices  11.1 us (20%)
  Pallas kernels  6.49 us (12%)
  local copies, waits for them, and re-layouts  2.06 us (4%)
  between operations  0.73 us (1%)
  other arithmetic  0.63 us (1%)
    all_to_all x1, blocking collectives, rotated(): lax.all_to_all(array, axis, 0, 0, tiled=True, axis_index_groups=[group])  21.1 us
    all_to_all x1, starting transfers between devices, rotated(): lax.all_to_all(array, axis, 0, 0, tiled=True, axis_index_groups=[group])  9.85 us
    all_to_all x1, waiting for transfers between devices, rotated(): lax.all_to_all(array, axis, 0, 0, tiled=True, axis_index_groups=[group])  9.82 us
    pallas_call x1, Pallas kernels, other_core(): pl.pallas_call(other_core_kernel, out_shape=shapes(((rows, heads * hd), F...  2.82 us
    pallas_call x1, Pallas kernels, own_block(): pl.pallas_call(own_kernel, out_shape=shapes(((heads * (rows + hd), hd), B...  2.29 us
    ppermute x1, starting transfers between devices, body(): b = lax.ppermute(a, CORE, [(0, 1), (1, 0)])  1.91 us
    pallas_call x1, Pallas kernels, same_core(): pl.pallas_call(same_core_kernel, out_shape=shapes(((steps, heads * rows,...  1.39 us
    ppermute x1, waiting for transfers between devices, body(): b = lax.ppermute(a, CORE, [(0, 1), (1, 0)])  1.23 us
  transfers between devices with their start and end apart: 2, of which 2 were waited for; matrix products, arithmetic and copies ran while one was open for 0% of the time, Pallas kernels for 7%

profile of v5, /device:TPU:24, one launch (start us, length us, event | category | flops | bytes accessed | tf_op | source)
XLA Modules:
  0.0 53.8 jit_solution(4805737654959185969)
XLA Ops:
  0.6 0.0 copy-start.3
  0.6 0.0 copy-start.2
  0.7 0.0 copy-start.1
  0.7 0.0 copy-start
  0.7 0.9 %constant_dynamic-slice_fusion = (bf16[128,128]{1,0:T(8,128)(2,1)S(1)}, bf16[128,128]{1,0:T(8,128)(2,1)S(1)}) fusion(bf16[128,1024]{1,0:T(8,128)(2,1)} %param.8, s32[]{:T(128)S(6)} %select_n.10, bf16[128,1024]{1,0:T(8,128)(2,1)} %param.7), kind=kLoop, calls=%fused_computation.2 | loop fusion | bytes 131076 | tf_op jit(solution)/shard_map/dynamic_slice | solution.py:274
  1.6 0.1 copy.11
  1.7 1.1 %broadcast_in_dim.3 = bf16[16,128,256]{2,1,0:T(8,128)(2,1)} broadcast(bf16[128,256]{1,0:T(8,128)(2,1)S(1)} %pad_maximum_fusion.kv_ref), dimensions={1,2} | broadcast | bytes 1114112 | tf_op jit(solution)/shard_map/broadcast_in_dim | solution.py:276
  2.8 9.9 %all-to-all-start = ((bf16[16,128,256]{2,1,0:T(8,128)(2,1)}), bf16[16,128,256]{2,1,0:T(8,128)(2,1)S(1)}, u32[]{:S(2)}, u32[]{:S(2)}) async-start(bf16[16,128,256]{2,1,0:T(8,128)(2,1)} %broadcast_in_dim.3), calls=%async_computation | async-start | bytes 2097152 | tf_op jit(solution)/shard_map/all_to_all | solution.py:202
  12.6 0.1 pad_add_fusion.at_ref
  12.7 0.0 copy-done.3
  12.7 0.0 copy-done.2
  12.7 0.0 copy-done.1
  12.7 0.0 copy-done
  12.7 2.3 %own_block.1 = (bf16[1024,128]{1,0:T(8,128)(2,1)S(1)}, f32[4,128,128]{2,1,0:T(8,128)S(1)}, f32[4,128,128]{2,1,0:T(8,128)S(1)}, bf16[4,128,256]{2,1,0:T(8,128)(2,...) custom-call(s32[2]{0:T(128)S(1)} %pad_add_fusion.at_ref, s32[12]{0:T(128)S(1)} %copy-done.3, ...), custom_call_target="tpu_custom_call" | custom-call | flops 1000000000 | bytes 2000000 | tf_op jit(solution)/shard_map/own_block/pallas_call | solution.py:216
  15.0 9.8 %all-to-all-done.a_ref = bf16[16,128,256]{2,1,0:T(8,128)(2,1)S(1)} async-done(((bf16[16,128,256]{2,1,0:T(8,128)(2,1)}), bf16[16,128,256]{2,1,0:T(8,128)(2,1)S(1)}, u32[]{:S(2)}, u32[]{:S(2)}) %all-to-all-start) | async-done | bytes 1048608 | tf_op jit(solution)/shard_map/all_to_all | solution.py:202
  24.8 1.9 %collective-permute-start = (bf16[16,128,256]{2,1,0:T(8,128)(2,1)S(1)}, bf16[16,128,256]{2,1,0:T(8,128)(2,1)S(1)}, u32[]{:S(2)}, u32[]{:S(2)}) collective-permute-start(bf16[16,128,256]{2,1,0:T(8,128)(2,1)S(1)} %all-to-all-done.a_ref), channel_id=1, source_target_pairs={{0,16},{16,0},{1,17},{17,1},{2,18},{18,2},{3,19},{19,3},{4,20},{20... | collective-permute-start | bytes 3145736 | tf_op jit(solution)/shard_map/ppermute | solution.py:280
  26.7 1.4 %same_core.1 = (f32[4,512,256]{2,1,0:T(8,128)S(1)}, f32[512,128]{1,0:T(8,128)S(1)}, f32[4,256,256]{2,1,0:T(8,128)S(1)}) custom-call(s32[2]{0:T(128)S(1)} %pad_add_fusion.at_ref, s32[12]{0:T(128)S(1)} %copy-done.3, bf16[16,128,256]{2,1,0:T(8,128)(2,1)S(1)} %all-to-all-done.a_ref, bf16[1024,128]{1,0:T(8,128)(2,1)S(1)} %get-tuple-element.17.lhs_ref), custom_call_target="tpu_custom_call" | custom-call | flops 2000000000 | bytes 4000000 | tf_op jit(solution)/shard_map/same_core/pallas_call | solution.py:237
  28.1 1.2 %collective-permute-done.b_ref = bf16[16,128,256]{2,1,0:T(8,128)(2,1)S(1)} collective-permute-done((bf16[16,128,256]{2,1,0:T(8,128)(2,1)S(1)}, bf16[16,128,256]{2,1,0:T(8,128)(2,1)S(1)}, u32[]{:S(2)}, u32[]{:S(2)}) %collective-permute-start) | collective-permute-done | bytes 1048608 | tf_op jit(solution)/shard_map/ppermute | solution.py:280
  29.4 2.8 %other_core.1 = (f32[128,512]{1,0:T(8,128)}, f32[16,128]{1,0:T(8,128)S(1)}) custom-call(s32[2]{0:T(128)S(1)} %pad_add_fusion.at_ref, s32[12]{0:T(128)S(1)} %copy-done.3, bf16[16,128,256]{2,1,0:T(8,128)(2,1)S(1)} %all-to-all-done.a_ref, bf16[16,128,256]{2,1,0:T(8,128)(2,1)S(1)} %collective-permute-done.b_ref, ...), custom_call_target="tpu_custom_call" | custom-call | flops 4000000000 | bytes 4000000 | tf_op jit(solution)/shard_map/other_core/pallas_call | solution.py:252
  32.2 21.1 %all_to_all.14 = f32[16,1,128]{2,1,0:T(1,128)S(1)} all-to-all(f32[16,1,128]{2,1,0:T(1,128)S(1)} %bitcast.6), channel_id=1, replica_groups={{10,11,12,13,14,15,0,1,2,3,4,5,6,7,8,9},{26,27,28,29,30,31,16,17,18,19,..., dimensions={0} | all-to-all | bytes 16384 | tf_op jit(solution)/shard_map/all_to_all | solution.py:202
  53.2 0.5 %reduce_sum.9 = f32[128]{0:T(128)} reduce(f32[16,1,128]{2,1,0:T(1,128)S(1)} %all_to_all.14, f32[]{:T(128)} %constant.44.clone.1), dimensions={0,1}, to_apply=%region_0.1 | reduce | flops 1920 | bytes 8708 | tf_op jit(solution)/shard_map/reduce_sum | solution.py:286
  (1 shorter events, 0.0 us)
Async XLA Ops:
  0.6 12.1 %copy-start.3 = (s32[12]{0:T(128)S(1)}, s32[12]{0:T(128)}, u32[]{:S(2)}) copy-start(s32[12]{0:T(128)} %doc_ref.5) | copy-start | bytes 148
  0.6 12.1 %copy-start.2 = (bf16[4,128,128]{2,1,0:T(8,128)(2,1)S(1)}, bf16[4,128,128]{2,1,0:T(8,128)(2,1)}, u32[]{:S(2)}) copy-start(bf16[4,128,128]{2,1,0:T(8,128)(2,1)} %fk_ref.1) | copy-start | bytes 393220
  0.7 12.1 %copy-start.1 = (bf16[4,128,128]{2,1,0:T(8,128)(2,1)S(1)}, bf16[4,128,128]{2,1,0:T(8,128)(2,1)}, u32[]{:S(2)}) copy-start(bf16[4,128,128]{2,1,0:T(8,128)(2,1)} %fq_ref.1) | copy-start | bytes 393220
  0.7 12.0 %copy-start = (bf16[128,512]{1,0:T(8,128)(2,1)S(1)}, bf16[128,512]{1,0:T(8,128)(2,1)}, u32[]{:S(2)}) copy-start(bf16[128,512]{1,0:T(8,128)(2,1)} %q_ref.1) | copy-start | bytes 393220
  2.8 22.1 %all-to-all-start = ((bf16[16,128,256]{2,1,0:T(8,128)(2,1)}), bf16[16,128,256]{2,1,0:T(8,128)(2,1)S(1)}, u32[]{:S(2)}, u32[]{:S(2)}) async-start(bf16[16,128,256]{2,1,0:T(8,128)(2,1)} %broadcast_in_dim.3), calls=%async_computation | async-start | bytes 2097152 | tf_op jit(solution)/shard_map/all_to_all | solution.py:202
  24.8 4.5 %collective-permute-start = (bf16[16,128,256]{2,1,0:T(8,128)(2,1)S(1)}, bf16[16,128,256]{2,1,0:T(8,128)(2,1)S(1)}, u32[]{:S(2)}, u32[]{:S(2)}) collective-permute-start(bf16[16,128,256]{2,1,0:T(8,128)(2,1)S(1)} %all-to-all-done.a_ref), channel_id=1, source_target_pairs={{0,16},{16,0},{1,17},{17,1},{2,18},{18,2},{3,19},{19,3},{4,20},{20... | collective-permute-start | bytes 3145736 | tf_op jit(solution)/shard_map/ppermute | solution.py:280

commit v6 on v5

--- a/solution.py
+++ b/solution.py
@@ -14,6 +14,8 @@
 CORE = "seq_2"
 SEQ = (*CHIP, CORE)
 NEG = -1e30
+MOST_KEY = 6.0
+LIMIT = 115.0
 FIRST_CHIP, FIRST_PLANE = 14, 10
 LOG2E = math.log2(math.e)
 
@@ -41,10 +43,13 @@
     return start
 
 
-def softmaxes(proj, axis):
+def softmaxes(proj, axis, small=False):
     p = proj * LOG2E
-    up = jnp.exp2(p - jnp.max(p, axis=axis, keepdims=True))
-    down = jnp.exp2(jnp.min(p, axis=axis, keepdims=True) - p)
+    if small:
+        up, down = jnp.exp2(p), jnp.exp2(-p)
+    else:
+        up = jnp.exp2(p - jnp.max(p, axis=axis, keepdims=True))
+        down = jnp.exp2(jnp.min(p, axis=axis, keepdims=True) - p)
     up = up * (1.0 / jnp.sum(up, axis=axis, keepdims=True))
     down = down * (1.0 / jnp.sum(down, axis=axis, keepdims=True))
     return jnp.concatenate([up.astype(jnp.bfloat16), down.astype(jnp.bfloat16)], axis=axis)
@@ -54,7 +59,7 @@
     return jnp.concatenate([v, jnp.ones_like(v)], axis=1)
 
 
-def own_kernel(at_ref, doc_ref, q_ref, kv_ref, fq_ref, fk_ref, lhs_ref, sd_ref, peak_ref, phi_ref, nd_ref, v_own_ref):
+def own_kernel(at_ref, doc_ref, q_ref, kv_ref, fq_ref, fk_ref, lhs_ref, sd_ref, peak_ref, phi_ref, nd_ref, v_own_ref, most_ref):
     heads, hd, _ = fq_ref.shape
     rows = q_ref.shape[0]
     anchor = (2 * at_ref[0] + at_ref[1]) * rows
@@ -64,10 +69,13 @@
     k_t = kv_ref[:, :rows]
     v = with_ones(kv_ref[:, rows:])
     v_own_ref[...] = v
+    most = jnp.zeros((hd, 1), jnp.float32)
     for h in range(heads):
         q = q_ref[:, h * hd:(h + 1) * hd]
         lhs_ref[h * rows:(h + 1) * rows, :] = q
-        fk_t = jnp.transpose(fk_ref[h].astype(jnp.float32)).astype(jnp.bfloat16)
+        fk_t = jnp.transpose(fk_ref[h].astype(jnp.float32))
+        most = jnp.maximum(most, jnp.sum(jnp.abs(fk_t), axis=1, keepdims=True))
+        fk_t = fk_t.astype(jnp.bfloat16)
         lhs_ref[heads * rows + h * hd:heads * rows + (h + 1) * hd, :] = fk_t
         sd = jnp.where(mask, dot(q, k_t) * (hd ** -0.5 * LOG2E), NEG)
         sd_ref[h] = sd
@@ -77,9 +85,10 @@
         phi_k = softmaxes(dot(fk_t, k_t), 0)
         affinity = jnp.where(mask, dot(phi_q, phi_k), 0.0)
         nd_ref[h] = split_dot(affinity, v)
-
-
-def scan_keys(kv_ref, lhs_ref, s_ref, max_ref, state_ref, c0, parity, first, anchor, before, skip):
+    most_ref[...] = jnp.full(most_ref.shape, jnp.max(most) * (MOST_KEY * LOG2E), jnp.float32)
+
+
+def scan_keys(kv_ref, lhs_ref, s_ref, max_ref, state_ref, c0, parity, first, anchor, before, skip, small):
     heads, rows, hd = state_ref.shape[0], max_ref.shape[1], kv_ref.shape[1]
     qr = heads * rows
     scale = hd ** -0.5 * LOG2E
@@ -105,7 +114,7 @@
         max_ref[...] = m
         v = with_ones(v) * jnp.where(visible(c, (2 * rows, 1), 0), 1.0, 0.0).astype(jnp.bfloat16)
         for h in range(heads):
-            d = dot(softmaxes(z[qr + h * hd:qr + (h + 1) * hd], 0), v)
+            d = dot(softmaxes(z[qr + h * hd:qr + (h + 1) * hd], 0, small), v)
             if i > skip:
                 d = state_ref[h] + d
             elif before is not None:
@@ -113,30 +122,31 @@
             state_ref[h] = d
 
 
-def as_far_as_needed(first, anchor, rows, steps, run):
-    skips = (steps - 1, steps // 2, 0)
-    nearer = False
-    for skip in skips:
+def as_far_as_needed(first, anchor, rows, steps, most, run):
+    small = most <= LIMIT
+    pl.when(jnp.logical_not(small))(functools.partial(run, 0, False))
+    left = small
+    for skip in (steps - 1, steps // 2, 0):
         reached = first >= anchor - 4 * (steps - skip) * rows if skip else True
-        pl.when(jnp.logical_and(reached, jnp.logical_not(nearer)))(functools.partial(run, skip))
-        nearer = jnp.logical_or(nearer, reached)
-
-
-def same_core_kernel(at_ref, doc_ref, a_ref, lhs_ref, s_ref, max_ref, state_ref):
+        pl.when(jnp.logical_and(left, reached))(functools.partial(run, skip, True))
+        left = jnp.logical_and(left, jnp.logical_not(reached))
+
+
+def same_core_kernel(at_ref, doc_ref, most_ref, a_ref, lhs_ref, s_ref, max_ref, state_ref):
     rows = max_ref.shape[1]
     chip, core = at_ref[0], at_ref[1]
     anchor = (2 * chip + core) * rows
     first = doc_start(doc_ref, anchor)
     steps = s_ref.shape[0]
 
-    def run(skip):
-        scan_keys(a_ref, lhs_ref, s_ref, max_ref, state_ref, chip - 2 * steps, core, first, anchor, None, skip)
-
-    as_far_as_needed(first, anchor, rows, steps, run)
+    def run(skip, small):
+        scan_keys(a_ref, lhs_ref, s_ref, max_ref, state_ref, chip - 2 * steps, core, first, anchor, None, skip, small)
+
+    as_far_as_needed(first, anchor, rows, steps, jnp.max(most_ref[0:1, 0:1]), run)
 
 
 def other_core_kernel(
-    at_ref, doc_ref, a_ref, b_ref, lhs_ref, sa_ref, max_a_ref, state_a_ref, sd_ref, peak_ref, phi_ref, nd_ref, v_own_ref,
+    at_ref, doc_ref, most_ref, a_ref, b_ref, lhs_ref, sa_ref, max_a_ref, state_a_ref, sd_ref, peak_ref, phi_ref, nd_ref, v_own_ref,
     res_ref, loss_ref, sb_ref, max_ref, state_ref, acc_ref,
 ):
     heads, rows, hd = sd_ref.shape
@@ -148,9 +158,9 @@
     q_pos = anchor + lax.broadcasted_iota(jnp.int32, (rows, 1), 0)
     carried = jnp.broadcast_to(jnp.where(doc_start(doc_ref, q_pos) == first, 1.0, 0.0), (rows, hd)) > 0.5
 
-    def run(skip):
+    def run(skip, small):
         before = (max_a_ref, state_a_ref)
-        scan_keys(b_ref, lhs_ref, sb_ref, max_ref, state_ref, b0, 1 - core, first, anchor, before, skip)
+        scan_keys(b_ref, lhs_ref, sb_ref, max_ref, state_ref, b0, 1 - core, first, anchor, before, skip, small)
         for h in range(heads):
             at = slice(h * rows, (h + 1) * rows)
             off = jnp.broadcast_to(jnp.max(max_ref[at], axis=1, keepdims=True), (rows, hd))
@@ -171,7 +181,7 @@
                 seen.append(with_ones(kv_ref[high, :, hd:]))
         acc_ref[...] += dot(jnp.concatenate(weights, axis=1), jnp.concatenate(seen, axis=0))
 
-    as_far_as_needed(first, anchor, rows, steps, run)
+    as_far_as_needed(first, anchor, rows, steps, jnp.max(most_ref[0:1, 0:1]), run)
 
     squares = jnp.zeros((rows, hd), jnp.float32)
     for h in range(heads):
@@ -222,16 +232,17 @@
             ((heads, rows, 2 * hd), BF16),
             ((heads, rows, 2 * hd), F32),
             ((rows, 2 * hd), BF16),
+            ((8, 128), F32),
         ),
         in_specs=[SMEM, SMEM] + [VMEM] * 4,
-        out_specs=(VMEM,) * 6,
+        out_specs=(VMEM,) * 7,
         compiler_params=params(16),
         cost_estimate=pl.CostEstimate(flops=10**9, bytes_accessed=2 * 10**6, transcendentals=10**6),
         name="own_block",
     )(at, doc_lengths, queries, kv_own, fq_weight, fk_weight)
 
 
-def same_core(at, doc_lengths, a, lhs, heads):
+def same_core(at, doc_lengths, most, a, lhs, heads):
     rows = hd = lhs.shape[1]
     steps = MAXDOC // (4 * rows)
     return pl.pallas_call(
@@ -239,20 +250,20 @@
         out_shape=shapes(
             ((steps, heads * rows, 2 * rows), F32), ((heads * rows, rows), F32), ((heads, 2 * hd, 2 * hd), F32)
         ),
-        in_specs=[SMEM, SMEM, VMEM, VMEM],
+        in_specs=[SMEM, SMEM, VMEM, VMEM, VMEM],
         out_specs=(VMEM,) * 3,
         compiler_params=params(16),
         cost_estimate=pl.CostEstimate(flops=2 * 10**9, bytes_accessed=4 * 10**6, transcendentals=2 * 10**6),
         name="same_core",
-    )(at, doc_lengths, a, lhs)
-
-
-def other_core(at, doc_lengths, a, b, lhs, sa, max_a, state_a, sd, peak, phi, nd, v_own, planes):
+    )(at, doc_lengths, most, a, lhs)
+
+
+def other_core(at, doc_lengths, most, a, b, lhs, sa, max_a, state_a, sd, peak, phi, nd, v_own, planes):
     heads, rows, hd = sd.shape
     return pl.pallas_call(
         other_core_kernel,
         out_shape=shapes(((rows, heads * hd), F32), ((planes, rows), F32)),
-        in_specs=[SMEM, SMEM] + [VMEM] * 11,
+        in_specs=[SMEM] * 2 + [VMEM] * 12,
         out_specs=(VMEM, VMEM),
         scratch_shapes=[
             pltpu.VMEM(sa.shape, F32),
@@ -263,7 +274,7 @@
         compiler_params=params(24),
         cost_estimate=pl.CostEstimate(flops=4 * 10**9, bytes_accessed=4 * 10**6, transcendentals=4 * 10**6),
         name="other_core",
-    )(at, doc_lengths, a, b, lhs, sa, max_a, state_a, sd, peak, phi, nd, v_own)
+    )(at, doc_lengths, most, a, b, lhs, sa, max_a, state_a, sd, peak, phi, nd, v_own)
 
 
 def body(queries, keys, values, doc_lengths, fq_weight, fk_weight):
@@ -275,12 +286,12 @@
     kv_own = jnp.concatenate([k_own.T, v_own], axis=1)
     send = jnp.broadcast_to(kv_own, (lax.axis_size(CHIP), *kv_own.shape))
     a = rotated(send, CHIP, FIRST_CHIP)
-    lhs, sd, peak, phi, nd, v_own = own_block(at, doc_lengths, queries, kv_own, fq_weight, fk_weight)
+    lhs, sd, peak, phi, nd, v_own, most = own_block(at, doc_lengths, queries, kv_own, fq_weight, fk_weight)
     a, lhs = lax.optimization_barrier((a, lhs))
     b = lax.ppermute(a, CORE, [(0, 1), (1, 0)])
-    sa, max_a, state_a = same_core(at, doc_lengths, a, lhs, heads)
+    sa, max_a, state_a = same_core(at, doc_lengths, most, a, lhs, heads)
     residual, loss = other_core(
-        at, doc_lengths, a, b, lhs, sa, max_a, state_a, sd, peak, phi, nd, v_own, lax.axis_size("head")
+        at, doc_lengths, most, a, b, lhs, sa, max_a, state_a, sd, peak, phi, nd, v_own, lax.axis_size("head")
     )
     parts = rotated(loss, "head", FIRST_PLANE)
     return residual, jnp.sum(parts, axis=0)

time: 54.5 us -> 56 us (1.028)
  Pallas kernels: 6.49 us -> 9.71 us
  waiting for transfers between devices: 11.1 us -> 9.82 us
    pallas_call x1, Pallas kernels: 2.82 us -> 4.8 us  [other_core(): pl.pallas_call(other_core_kernel, out_shape=shapes(((rows, heads * hd), F...]
    ppermute x1, waiting for transfers between devices: 1.23 us -> 0.01 us  [body(): b = lax.ppermute(a, CORE, [(0, 1), (1, 0)])]
    pallas_call x1, Pallas kernels: 1.39 us -> 2.61 us  [same_core(): pl.pallas_call(same_core_kernel, out_shape=shapes(((steps, heads * rows,...]
  transfers between devices with their start and end apart: 2 -> 2, of which waited for: 2 -> 1; matrix products, arithmetic and copies ran while one was open for 0% -> 0% of each run, Pallas kernels for 7% -> 9%
where the time goes in v6:
time: 56 us; the launch traced here: 55.7 us
  blocking collectives  21 us (38%)
  starting transfers between devices  11.8 us (21%)
  waiting for transfers between devices  9.82 us (18%)
  Pallas kernels  9.71 us (17%)
  local copies, waits for them, and re-layouts  2.06 us (4%)
  between operations  0.73 us (1%)
  other arithmetic  0.63 us (1%)
    all_to_all x1, blocking collectives, rotated(): lax.all_to_all(array, axis, 0, 0, tiled=True, axis_index_groups=[group])  21 us
    all_to_all x1, starting transfers between devices, rotated(): lax.all_to_all(array, axis, 0, 0, tiled=True, axis_index_groups=[group])  9.85 us
    all_to_all x1, waiting for transfers between devices, rotated(): lax.all_to_all(array, axis, 0, 0, tiled=True, axis_index_groups=[group])  9.82 us
    pallas_call x1, Pallas kernels, other_core(): pl.pallas_call(other_core_kernel, out_shape=shapes(((rows, heads * hd), F...  4.8 us
    pallas_call x1, Pallas kernels, same_core(): pl.pallas_call(same_core_kernel, out_shape=shapes(((steps, heads * rows,...  2.61 us
    pallas_call x1, Pallas kernels, own_block(): pl.pallas_call(own_kernel, out_shape=shapes(((heads * (rows + hd), hd), B...  2.29 us
    ppermute x1, starting transfers between devices, body(): b = lax.ppermute(a, CORE, [(0, 1), (1, 0)])  1.91 us
  transfers between devices with their start and end apart: 2, of which 1 were waited for; matrix products, arithmetic and copies ran while one was open for 0% of the time, Pallas kernels for 9%

profile of v6, /device:TPU:24, one launch (start us, length us, event | category | flops | bytes accessed | tf_op | source)
XLA Modules:
  0.0 55.7 jit_solution(16808539103455747775)
XLA Ops:
  0.6 0.0 copy-start.3
  0.6 0.0 copy-start.2
  0.7 0.0 copy-start.1
  0.7 0.0 copy-start
  0.7 0.9 %constant_dynamic-slice_fusion = (bf16[128,128]{1,0:T(8,128)(2,1)S(1)}, bf16[128,128]{1,0:T(8,128)(2,1)S(1)}) fusion(bf16[128,1024]{1,0:T(8,128)(2,1)} %param.8, s32[]{:T(128)S(6)} %select_n.10, bf16[128,1024]{1,0:T(8,128)(2,1)} %param.7), kind=kLoop, calls=%fused_computation.2 | loop fusion | bytes 131076 | tf_op jit(solution)/shard_map/dynamic_slice | solution.py:285
  1.6 0.1 copy.11
  1.7 1.1 %broadcast_in_dim.3 = bf16[16,128,256]{2,1,0:T(8,128)(2,1)} broadcast(bf16[128,256]{1,0:T(8,128)(2,1)S(1)} %pad_maximum_fusion.kv_ref), dimensions={1,2} | broadcast | bytes 1114112 | tf_op jit(solution)/shard_map/broadcast_in_dim | solution.py:287
  2.8 9.9 %all-to-all-start = ((bf16[16,128,256]{2,1,0:T(8,128)(2,1)}), bf16[16,128,256]{2,1,0:T(8,128)(2,1)S(1)}, u32[]{:S(2)}, u32[]{:S(2)}) async-start(bf16[16,128,256]{2,1,0:T(8,128)(2,1)} %broadcast_in_dim.3), calls=%async_computation | async-start | bytes 2097152 | tf_op jit(solution)/shard_map/all_to_all | solution.py:212
  12.6 0.1 pad_add_fusion.at_ref
  12.7 0.0 copy-done.3
  12.7 0.0 copy-done.2
  12.7 0.0 copy-done.1
  12.7 0.0 copy-done
  12.7 2.3 %own_block.1 = (bf16[1024,128]{1,0:T(8,128)(2,1)S(1)}, f32[4,128,128]{2,1,0:T(8,128)S(1)}, f32[4,128,128]{2,1,0:T(8,128)S(1)}, bf16[4,128,256]{2,1,0:T(8,128)(2,...) custom-call(s32[2]{0:T(128)S(1)} %pad_add_fusion.at_ref, s32[12]{0:T(128)S(1)} %copy-done.3, ...), custom_call_target="tpu_custom_call" | custom-call | flops 1000000000 | bytes 2000000 | tf_op jit(solution)/shard_map/own_block/pallas_call | solution.py:226
  15.0 9.8 %all-to-all-done.a_ref = bf16[16,128,256]{2,1,0:T(8,128)(2,1)S(1)} async-done(((bf16[16,128,256]{2,1,0:T(8,128)(2,1)}), bf16[16,128,256]{2,1,0:T(8,128)(2,1)S(1)}, u32[]{:S(2)}, u32[]{:S(2)}) %all-to-all-start) | async-done | bytes 1048608 | tf_op jit(solution)/shard_map/all_to_all | solution.py:212
  24.8 1.9 %collective-permute-start = (bf16[16,128,256]{2,1,0:T(8,128)(2,1)S(1)}, bf16[16,128,256]{2,1,0:T(8,128)(2,1)S(1)}, u32[]{:S(2)}, u32[]{:S(2)}) collective-permute-start(bf16[16,128,256]{2,1,0:T(8,128)(2,1)S(1)} %all-to-all-done.a_ref), channel_id=1, source_target_pairs={{0,16},{16,0},{1,17},{17,1},{2,18},{18,2},{3,19},{19,3},{4,20},{20... | collective-permute-start | bytes 3145736 | tf_op jit(solution)/shard_map/ppermute | solution.py:291
  26.7 2.6 %same_core.1 = (f32[4,512,256]{2,1,0:T(8,128)S(1)}, f32[512,128]{1,0:T(8,128)S(1)}, f32[4,256,256]{2,1,0:T(8,128)S(1)}) custom-call(s32[2]{0:T(128)S(1)} %pad_add_fusion.at_ref, s32[12]{0:T(128)S(1)} %copy-done.3, f32[8,128]{1,0:T(8,128)S(1)} %get-tuple-element.16.most_ref, bf16[16,128,256]{2,1,0:T(8,128)(2,1)S(1)} %all-to-all-done.a_ref, ...), custom_call_target="tpu_custom_call" | custom-call | flops 2000000000 | bytes 4000000 | tf_op jit(solution)/shard_map/same_core/pallas_call | solution.py:248
  29.4 0.0 collective-permute-done.b_ref
  29.4 4.8 %other_core.1 = (f32[128,512]{1,0:T(8,128)}, f32[16,128]{1,0:T(8,128)S(1)}) custom-call(s32[2]{0:T(128)S(1)} %pad_add_fusion.at_ref, s32[12]{0:T(128)S(1)} %copy-done.3, f32[8,128]{1,0:T(8,128)S(1)} %get-tuple-element.16.most_ref, bf16[16,128,256]{2,1,0:T(8,128)(2,1)S(1)} %all-to-all-done.a_ref, bf16[16,128,256]{2,1,0:T(8,128)(2,1)S(1)} %collective-permute-done.b_ref, ...), custom_call_target="tpu_custom_call" | custom-call | flops 4000000000 | bytes 4000000 | tf_op jit(solution)/shard_map/other_core/pallas_call | solution.py:263
  34.2 21.0 %all_to_all.14 = f32[16,1,128]{2,1,0:T(1,128)S(1)} all-to-all(f32[16,1,128]{2,1,0:T(1,128)S(1)} %bitcast.6), channel_id=1, replica_groups={{10,11,12,13,14,15,0,1,2,3,4,5,6,7,8,9},{26,27,28,29,30,31,16,17,18,19,..., dimensions={0} | all-to-all | bytes 16384 | tf_op jit(solution)/shard_map/all_to_all | solution.py:212
  55.2 0.5 reduce_sum.9
  (1 shorter events, 0.0 us)
Async XLA Ops:
  0.6 12.1 %copy-start.3 = (s32[12]{0:T(128)S(1)}, s32[12]{0:T(128)}, u32[]{:S(2)}) copy-start(s32[12]{0:T(128)} %doc_ref.5) | copy-start | bytes 148
  0.6 12.1 %copy-start.2 = (bf16[4,128,128]{2,1,0:T(8,128)(2,1)S(1)}, bf16[4,128,128]{2,1,0:T(8,128)(2,1)}, u32[]{:S(2)}) copy-start(bf16[4,128,128]{2,1,0:T(8,128)(2,1)} %fk_ref.1) | copy-start | bytes 393220
  0.7 12.1 %copy-start.1 = (bf16[4,128,128]{2,1,0:T(8,128)(2,1)S(1)}, bf16[4,128,128]{2,1,0:T(8,128)(2,1)}, u32[]{:S(2)}) copy-start(bf16[4,128,128]{2,1,0:T(8,128)(2,1)} %fq_ref.1) | copy-start | bytes 393220
  0.7 12.0 %copy-start = (bf16[128,512]{1,0:T(8,128)(2,1)S(1)}, bf16[128,512]{1,0:T(8,128)(2,1)}, u32[]{:S(2)}) copy-start(bf16[128,512]{1,0:T(8,128)(2,1)} %q_ref.1) | copy-start | bytes 393220
  2.8 22.1 %all-to-all-start = ((bf16[16,128,256]{2,1,0:T(8,128)(2,1)}), bf16[16,128,256]{2,1,0:T(8,128)(2,1)S(1)}, u32[]{:S(2)}, u32[]{:S(2)}) async-start(bf16[16,128,256]{2,1,0:T(8,128)(2,1)} %broadcast_in_dim.3), calls=%async_computation | async-start | bytes 2097152 | tf_op jit(solution)/shard_map/all_to_all | solution.py:212
  24.8 4.5 %collective-permute-start = (bf16[16,128,256]{2,1,0:T(8,128)(2,1)S(1)}, bf16[16,128,256]{2,1,0:T(8,128)(2,1)S(1)}, u32[]{:S(2)}, u32[]{:S(2)}) collective-permute-start(bf16[16,128,256]{2,1,0:T(8,128)(2,1)S(1)} %all-to-all-done.a_ref), channel_id=1, source_target_pairs={{0,16},{16,0},{1,17},{17,1},{2,18},{18,2},{3,19},{19,3},{4,20},{20... | collective-permute-start | bytes 3145736 | tf_op jit(solution)/shard_map/ppermute | solution.py:291

commit v7 on v6

--- a/solution.py
+++ b/solution.py
@@ -98,13 +98,17 @@
         pos = (2 * c + parity) * rows + lane + jnp.where(lane < rows, 0, rows)
         return (pos >= first) & (pos < anchor)
 
-    for i in range(skip, s_ref.shape[0]):
+    steps = s_ref.shape[0]
+    whole = {0: steps // 2, steps // 2: steps - 1}.get(skip, steps) if small else steps
+    for i in range(skip, steps):
         c = c0 + 2 * i
         low, high = slot(c, kv_ref.shape[0]), slot(c + 1, kv_ref.shape[0])
         k_t = jnp.concatenate([kv_ref[low, :, :hd], kv_ref[high, :, :hd]], axis=1)
         v = jnp.concatenate([kv_ref[low, :, hd:], kv_ref[high, :, hd:]], axis=0)
         z = dot(lhs_ref[...], k_t)
-        s = jnp.where(visible(c, (1, 2 * rows), 1), z[:qr] * scale, NEG)
+        s = z[:qr] * scale
+        if i < whole:
+            s = jnp.where(visible(c, (1, 2 * rows), 1), s, NEG)
         s_ref[i] = s
         m = jnp.maximum(s[:, :rows], s[:, rows:])
         if i > skip:
@@ -112,7 +116,9 @@
         elif before is not None:
             m = jnp.maximum(before[0][...], m)
         max_ref[...] = m
-        v = with_ones(v) * jnp.where(visible(c, (2 * rows, 1), 0), 1.0, 0.0).astype(jnp.bfloat16)
+        v = with_ones(v)
+        if i < whole:
+            v = v * jnp.where(visible(c, (2 * rows, 1), 0), 1.0, 0.0).astype(jnp.bfloat16)
         for h in range(heads):
             d = dot(softmaxes(z[qr + h * hd:qr + (h + 1) * hd], 0, small), v)
             if i > skip:

time: 56 us -> 56 us (level)
  no operation moved by 1% of the time
where the time goes in v7:
time: 56 us; the launch traced here: 55.7 us
  blocking collectives  21 us (38%)
  starting transfers between devices  11.8 us (21%)
  waiting for transfers between devices  9.83 us (18%)
  Pallas kernels  9.67 us (17%)
  local copies, waits for them, and re-layouts  2.06 us (4%)
  between operations  0.73 us (1%)
  other arithmetic  0.63 us (1%)
    all_to_all x1, blocking collectives, rotated(): lax.all_to_all(array, axis, 0, 0, tiled=True, axis_index_groups=[group])  21 us
    all_to_all x1, starting transfers between devices, rotated(): lax.all_to_all(array, axis, 0, 0, tiled=True, axis_index_groups=[group])  9.85 us
    all_to_all x1, waiting for transfers between devices, rotated(): lax.all_to_all(array, axis, 0, 0, tiled=True, axis_index_groups=[group])  9.82 us
    pallas_call x1, Pallas kernels, other_core(): pl.pallas_call(other_core_kernel, out_shape=shapes(((rows, heads * hd), F...  4.77 us
    pallas_call x1, Pallas kernels, same_core(): pl.pallas_call(same_core_kernel, out_shape=shapes(((steps, heads * rows,...  2.6 us
    pallas_call x1, Pallas kernels, own_block(): pl.pallas_call(own_kernel, out_shape=shapes(((heads * (rows + hd), hd), B...  2.29 us
    ppermute x1, starting transfers between devices, body(): b = lax.ppermute(a, CORE, [(0, 1), (1, 0)])  1.91 us
  transfers between devices with their start and end apart: 2, of which 1 were waited for; matrix products, arithmetic and copies ran while one was open for 0% of the time, Pallas kernels for 9%

profile of v7, /device:TPU:24, one launch (start us, length us, event | category | flops | bytes accessed | tf_op | source)
XLA Modules:
  0.0 55.7 jit_solution(13060780663409451929)
XLA Ops:
  0.6 0.0 copy-start.3
  0.6 0.0 copy-start.2
  0.7 0.0 copy-start.1
  0.7 0.0 copy-start
  0.7 0.9 %constant_dynamic-slice_fusion = (bf16[128,128]{1,0:T(8,128)(2,1)S(1)}, bf16[128,128]{1,0:T(8,128)(2,1)S(1)}) fusion(bf16[128,1024]{1,0:T(8,128)(2,1)} %param.8, s32[]{:T(128)S(6)} %select_n.10, bf16[128,1024]{1,0:T(8,128)(2,1)} %param.7), kind=kLoop, calls=%fused_computation.2 | loop fusion | bytes 131076 | tf_op jit(solution)/shard_map/dynamic_slice | solution.py:291
  1.6 0.1 copy.11
  1.7 1.1 %broadcast_in_dim.3 = bf16[16,128,256]{2,1,0:T(8,128)(2,1)} broadcast(bf16[128,256]{1,0:T(8,128)(2,1)S(1)} %pad_maximum_fusion.kv_ref), dimensions={1,2} | broadcast | bytes 1114112 | tf_op jit(solution)/shard_map/broadcast_in_dim | solution.py:293
  2.8 9.9 %all-to-all-start = ((bf16[16,128,256]{2,1,0:T(8,128)(2,1)}), bf16[16,128,256]{2,1,0:T(8,128)(2,1)S(1)}, u32[]{:S(2)}, u32[]{:S(2)}) async-start(bf16[16,128,256]{2,1,0:T(8,128)(2,1)} %broadcast_in_dim.3), calls=%async_computation | async-start | bytes 2097152 | tf_op jit(solution)/shard_map/all_to_all | solution.py:218
  12.6 0.1 pad_add_fusion.at_ref
  12.7 0.0 copy-done.3
  12.7 0.0 copy-done.2
  12.7 0.0 copy-done.1
  12.7 0.0 copy-done
  12.7 2.3 %own_block.1 = (bf16[1024,128]{1,0:T(8,128)(2,1)S(1)}, f32[4,128,128]{2,1,0:T(8,128)S(1)}, f32[4,128,128]{2,1,0:T(8,128)S(1)}, bf16[4,128,256]{2,1,0:T(8,128)(2,...) custom-call(s32[2]{0:T(128)S(1)} %pad_add_fusion.at_ref, s32[12]{0:T(128)S(1)} %copy-done.3, ...), custom_call_target="tpu_custom_call" | custom-call | flops 1000000000 | bytes 2000000 | tf_op jit(solution)/shard_map/own_block/pallas_call | solution.py:232
  15.0 9.8 %all-to-all-done.a_ref = bf16[16,128,256]{2,1,0:T(8,128)(2,1)S(1)} async-done(((bf16[16,128,256]{2,1,0:T(8,128)(2,1)}), bf16[16,128,256]{2,1,0:T(8,128)(2,1)S(1)}, u32[]{:S(2)}, u32[]{:S(2)}) %all-to-all-start) | async-done | bytes 1048608 | tf_op jit(solution)/shard_map/all_to_all | solution.py:218
  24.8 1.9 %collective-permute-start = (bf16[16,128,256]{2,1,0:T(8,128)(2,1)S(1)}, bf16[16,128,256]{2,1,0:T(8,128)(2,1)S(1)}, u32[]{:S(2)}, u32[]{:S(2)}) collective-permute-start(bf16[16,128,256]{2,1,0:T(8,128)(2,1)S(1)} %all-to-all-done.a_ref), channel_id=1, source_target_pairs={{0,16},{16,0},{1,17},{17,1},{2,18},{18,2},{3,19},{19,3},{4,20},{20... | collective-permute-start | bytes 3145736 | tf_op jit(solution)/shard_map/ppermute | solution.py:297
  26.7 2.6 %same_core.1 = (f32[4,512,256]{2,1,0:T(8,128)S(1)}, f32[512,128]{1,0:T(8,128)S(1)}, f32[4,256,256]{2,1,0:T(8,128)S(1)}) custom-call(s32[2]{0:T(128)S(1)} %pad_add_fusion.at_ref, s32[12]{0:T(128)S(1)} %copy-done.3, f32[8,128]{1,0:T(8,128)S(1)} %get-tuple-element.16.most_ref, bf16[16,128,256]{2,1,0:T(8,128)(2,1)S(1)} %all-to-all-done.a_ref, ...), custom_call_target="tpu_custom_call" | custom-call | flops 2000000000 | bytes 4000000 | tf_op jit(solution)/shard_map/same_core/pallas_call | solution.py:254
  29.4 0.0 collective-permute-done.b_ref
  29.4 4.8 %other_core.1 = (f32[128,512]{1,0:T(8,128)}, f32[16,128]{1,0:T(8,128)S(1)}) custom-call(s32[2]{0:T(128)S(1)} %pad_add_fusion.at_ref, s32[12]{0:T(128)S(1)} %copy-done.3, f32[8,128]{1,0:T(8,128)S(1)} %get-tuple-element.16.most_ref, bf16[16,128,256]{2,1,0:T(8,128)(2,1)S(1)} %all-to-all-done.a_ref, bf16[16,128,256]{2,1,0:T(8,128)(2,1)S(1)} %collective-permute-done.b_ref, ...), custom_call_target="tpu_custom_call" | custom-call | flops 4000000000 | bytes 4000000 | tf_op jit(solution)/shard_map/other_core/pallas_call | solution.py:269
  34.1 21.0 %all_to_all.14 = f32[16,1,128]{2,1,0:T(1,128)S(1)} all-to-all(f32[16,1,128]{2,1,0:T(1,128)S(1)} %bitcast.6), channel_id=1, replica_groups={{10,11,12,13,14,15,0,1,2,3,4,5,6,7,8,9},{26,27,28,29,30,31,16,17,18,19,..., dimensions={0} | all-to-all | bytes 16384 | tf_op jit(solution)/shard_map/all_to_all | solution.py:218
  55.2 0.5 reduce_sum.9
  (1 shorter events, 0.0 us)
Async XLA Ops:
  0.6 12.1 %copy-start.3 = (s32[12]{0:T(128)S(1)}, s32[12]{0:T(128)}, u32[]{:S(2)}) copy-start(s32[12]{0:T(128)} %doc_ref.5) | copy-start | bytes 148
  0.6 12.1 %copy-start.2 = (bf16[4,128,128]{2,1,0:T(8,128)(2,1)S(1)}, bf16[4,128,128]{2,1,0:T(8,128)(2,1)}, u32[]{:S(2)}) copy-start(bf16[4,128,128]{2,1,0:T(8,128)(2,1)} %fk_ref.1) | copy-start | bytes 393220
  0.7 12.1 %copy-start.1 = (bf16[4,128,128]{2,1,0:T(8,128)(2,1)S(1)}, bf16[4,128,128]{2,1,0:T(8,128)(2,1)}, u32[]{:S(2)}) copy-start(bf16[4,128,128]{2,1,0:T(8,128)(2,1)} %fq_ref.1) | copy-start | bytes 393220
  0.7 12.0 %copy-start = (bf16[128,512]{1,0:T(8,128)(2,1)S(1)}, bf16[128,512]{1,0:T(8,128)(2,1)}, u32[]{:S(2)}) copy-start(bf16[128,512]{1,0:T(8,128)(2,1)} %q_ref.1) | copy-start | bytes 393220
  2.8 22.1 %all-to-all-start = ((bf16[16,128,256]{2,1,0:T(8,128)(2,1)}), bf16[16,128,256]{2,1,0:T(8,128)(2,1)S(1)}, u32[]{:S(2)}, u32[]{:S(2)}) async-start(bf16[16,128,256]{2,1,0:T(8,128)(2,1)} %broadcast_in_dim.3), calls=%async_computation | async-start | bytes 2097152 | tf_op jit(solution)/shard_map/all_to_all | solution.py:218
  24.8 4.5 %collective-permute-start = (bf16[16,128,256]{2,1,0:T(8,128)(2,1)S(1)}, bf16[16,128,256]{2,1,0:T(8,128)(2,1)S(1)}, u32[]{:S(2)}, u32[]{:S(2)}) collective-permute-start(bf16[16,128,256]{2,1,0:T(8,128)(2,1)S(1)} %all-to-all-done.a_ref), channel_id=1, source_target_pairs={{0,16},{16,0},{1,17},{17,1},{2,18},{18,2},{3,19},{19,3},{4,20},{20... | collective-permute-start | bytes 3145736 | tf_op jit(solution)/shard_map/ppermute | solution.py:297
